TPU v7x, 512 devices: a whole 4x4x16 slice. The times are simulated.
512 devices in a mesh: attn: 16 (over x, z_lo), ffn: 4 (over z_hi), tp: 8 (over y, core).
Axes of the slice: x: 4, y: 4, z: 16 (z_hi: 4, z_lo: 4; z = z_hi * 4 + z_lo), core: 2. Of those that a mesh axis runs over, the one named last changes fastest.
Arguments:
- x_init: bfloat16 [192, 8192], P(('attn', 'ffn'), 'tp'), may hold values from -14 to 14
- queries: bfloat16 [3, 192, 64, 128], P(None, ('attn', 'ffn'), 'tp'), may hold values from -120 to 120
- new_kv: bfloat16 [3, 192, 8, 2, 128], P(None, ('attn', 'ffn'), 'tp'), may hold values from -6 to 6
- kv_cache: bfloat16 [192, 8, 2, 1024, 128], P(('attn', 'ffn'), 'tp'), may hold values from -6 to 6
- lengths: int32 [192], P(('attn', 'ffn')), may hold values from 2 to 1024, as said below
- norm_gain: bfloat16 [8192], P('tp'), may hold values from 0.099609375 to 1.8984375
- w_gate_up: bfloat16 [8192, 2, 32768], P('tp', None, ('attn', 'ffn')), may hold values from -0.0625 to 0.0625
- w_down: bfloat16 [32768, 8192], P(('attn', 'ffn'), 'tp'), may hold values from -0.03125 to 0.03125
Outputs:
- outputs: bfloat16 [3, 192, 8192], P(None, ('attn', 'ffn'), 'tp')
Inputs may be any that keep to these rules, and one draw needn't show every extreme that they name: `lengths`: every request has 2 or more live positions; the largest length is exactly 1024.
All inputs are finite; a program needn't handle non-finite values.
Results may differ from a plain program's by a relative error of at most 0.024.
Values may be sent and summed in bfloat16 or wider, within the bound.
No kernel may reach another device: no remote copies, remote signals or barrier semaphores. Data moves between devices by JAX's collectives and lax.ppermute only.
A program may use at most 64 MiB of HBM per device.

v0:
```python
import jax
import jax.numpy as jnp
from jax import lax
from jax.sharding import PartitionSpec as P

D = 8192


def on_device(x_init, queries, new_kv, kv_cache, lengths, norm_gain, w_gate_up, w_down):
    requests = x_init.shape[0]
    local_width = x_init.shape[1]
    steps_total = queries.shape[0]
    head_count = queries.shape[2]
    head_size = queries.shape[3]
    kv_count = kv_cache.shape[1]
    group_size = head_count // kv_count
    cache_length = kv_cache.shape[3]
    hidden_local = w_gate_up.shape[2]
    weight_flat = w_gate_up.reshape(local_width, 2 * hidden_local)
    score_scale = head_size ** (-0.5)
    cache_keys = kv_cache[:, :, 0]
    cache_values = kv_cache[:, :, 1]
    live_mask = jnp.arange(cache_length, dtype=jnp.int32)[None, :] < lengths[:, None]
    gain_values = norm_gain.astype(jnp.float32)
    state = x_init
    results = []
    for step_index in range(steps_total):
        grouped = queries[step_index].reshape(requests, kv_count, group_size, head_size)
        cache_scores = (
            jnp.einsum("rkgd,rkld->rkgl", grouped, cache_keys, preferred_element_type=jnp.float32)
            * score_scale
        )
        cache_scores = jnp.where(live_mask[:, None, None, :], cache_scores, -1e30)
        fresh_keys = new_kv[: step_index + 1, :, :, 0]
        fresh_values = new_kv[: step_index + 1, :, :, 1]
        fresh_scores = (
            jnp.einsum("rkgd,nrkd->rkgn", grouped, fresh_keys, preferred_element_type=jnp.float32)
            * score_scale
        )
        row_max = jnp.maximum(jnp.max(cache_scores, axis=-1), jnp.max(fresh_scores, axis=-1))[
            ..., None
        ]
        cache_exp = jnp.exp(cache_scores - row_max)
        fresh_exp = jnp.exp(fresh_scores - row_max)
        exp_total = jnp.sum(cache_exp, axis=-1, keepdims=True) + jnp.sum(
            fresh_exp, axis=-1, keepdims=True
        )
        cache_probs = (cache_exp / exp_total).astype(jnp.bfloat16)
        fresh_probs = (fresh_exp / exp_total).astype(jnp.bfloat16)
        attended = jnp.einsum(
            "rkgl,rkld->rkgd", cache_probs, cache_values, preferred_element_type=jnp.float32
        )
        attended = attended + jnp.einsum(
            "rkgn,nrkd->rkgd", fresh_probs, fresh_values, preferred_element_type=jnp.float32
        )
        hidden_in = state.astype(jnp.float32) + attended.reshape(requests, local_width)
        squares = lax.psum(jnp.sum(hidden_in * hidden_in, axis=1), "tp")
        inv_rms = lax.rsqrt(squares / D + 1e-05)
        normed = (hidden_in * inv_rms[:, None] * gain_values).astype(jnp.bfloat16)
        partial_sums = jnp.dot(
            lax.all_gather(normed, ("attn", "ffn"), axis=0, tiled=True),
            weight_flat,
            preferred_element_type=jnp.float32,
        )
        summed = lax.psum(partial_sums.astype(jnp.bfloat16), "tp").astype(jnp.float32)
        hidden = (jax.nn.silu(summed[:, :hidden_local]) * summed[:, hidden_local:]).astype(
            jnp.bfloat16
        )
        returned = lax.psum_scatter(
            jnp.dot(hidden, w_down, preferred_element_type=jnp.float32),
            ("attn", "ffn"),
            scatter_dimension=0,
            tiled=True,
        )
        state = (hidden_in + returned).astype(jnp.bfloat16)
        results.append(state)
    return jnp.stack(results)


def solution(mesh):
    return jax.shard_map(
        on_device,
        mesh=mesh,
        in_specs=(
            P(("attn", "ffn"), "tp"),
            P(None, ("attn", "ffn"), "tp", None),
            P(None, ("attn", "ffn"), "tp", None, None),
            P(("attn", "ffn"), "tp", None, None, None),
            P(("attn", "ffn")),
            P("tp"),
            P("tp", None, ("attn", "ffn")),
            P(("attn", "ffn"), "tp"),
        ),
        out_specs=P(None, ("attn", "ffn"), "tp"),
        check_vma=False,
    )
```

profile of v0, /device:TPU:32, one launch (start us, length us, event | category | flops | bytes accessed | tf_op | source)
XLA Modules:
  0.0 1613.5 jit_solution(3175260596030056903)
XLA Ops:
  6.5 0.8 iota_compare_fusion
  7.4 0.7 slice_convert_fusion
  8.0 0.8 fusion.51
  8.9 1.5 fusion.83
  10.4 0.2 fusion.31
  10.6 1.4 fusion.5
  12.0 0.0 copy-start.4
  12.0 0.1 multiply_reduce_fusion.2
  12.2 14.9 psum.42
  27.1 0.1 fusion.43
  27.1 172.6 %all-gather = bf16[64,3,1024]{2,1,0:T(4,128)(2,1)S(1)} all-gather(bf16[1,3,1024]{2,1,0:T(4,128)(2,1)S(1)} %fusion.43), channel_id=1, replica_groups=mesh['attn'=16,'ffn'=4,'tp'=8] {'attn','ffn'}, dimensions={0}, use_global_device_ids=true | all-gather | bytes 399360 | tf_op jit(solution)/shard_map/all_gather | solution.py:61
  199.8 0.3 reshape.270
  200.1 2.2 copy.37
  202.3 1.3 convolution_convert_fusion.2
  203.6 0.0 all-reduce.10.cloned.1.call-update
  203.6 0.0 all-reduce.16.cloned.1.call-start
  203.7 1.5 fusion.81
  205.2 0.8 fusion.77
  206.0 0.8 fusion.82
  206.8 65.5 %all-reduce.10.cloned.1.call-done = bf16[192,1024]{1,0:T(8,128)(2,1)} async-done(((bf16[192,1024]{1,0:T(8,128)(2,1)}), bf16[192,1024]{1,0:T(8,128)(2,1)}) %all-reduce.10.cloned.1.call-update) | async-done | bytes 393232 | tf_op jit(solution)/shard_map/psum | solution.py:65
  272.3 1.1 convert_element_type.87
  273.4 1.3 fusion.22
  274.7 0.0 all-reduce.16.cloned.1.call-update
  274.7 0.0 all-reduce.12.cloned.1.call-start
  274.8 0.2 fusion.32
  275.0 1.3 dynamic-slice
  276.9 0.2 fusion.65
  277.1 1.4 fusion.4
  278.5 2.7 fusion.79
  281.2 262.1 %all-reduce.16.cloned.1.call-done = f32[192,1024]{1,0:T(8,128)} async-done(((f32[192,1024]{1,0:T(8,128)}), f32[192,1024]{1,0:T(8,128)}) %all-reduce.16.cloned.1.call-update) | async-done | bytes 786448
  543.3 1.0 multiply_reduce_fusion.1
  544.3 12.4 psum.44
  556.7 0.1 fusion.44
  556.8 175.8 %all-gather.1 = bf16[64,3,1024]{2,1,0:T(4,128)(2,1)} all-gather(bf16[1,3,1024]{2,1,0:T(4,128)(2,1)S(1)} %fusion.44), channel_id=1, replica_groups=mesh['attn'=16,'ffn'=4,'tp'=8] {'attn','ffn'}, dimensions={0}, use_global_device_ids=true | all-gather | bytes 399360 | tf_op jit(solution)/shard_map/all_gather | solution.py:61
  732.7 1.4 reshape.272
  734.1 0.0 copy-start.12
  734.1 1.3 convolution_convert_fusion.1
  735.4 0.0 all-reduce.12.cloned.1.call-update
  735.4 0.0 all-reduce.18.cloned.1.call-start
  735.5 67.9 %all-reduce.12.cloned.1.call-done = bf16[192,1024]{1,0:T(8,128)(2,1)} async-done(((bf16[192,1024]{1,0:T(8,128)(2,1)}), bf16[192,1024]{1,0:T(8,128)(2,1)}) %all-reduce.12.cloned.1.call-update) | async-done | bytes 393232 | tf_op jit(solution)/shard_map/psum | solution.py:65
  803.4 1.1 convert_element_type.95
  804.5 1.3 fusion.24
  805.8 0.0 all-reduce.18.cloned.1.call-update
  805.8 0.0 all-reduce.14.cloned.1.call-start
  805.9 0.8 fusion.80
  806.8 0.2 fusion.33
  806.9 1.4 fusion.6
  808.3 0.2 fusion.3
  808.6 265.7 %all-reduce.18.cloned.1.call-done = f32[192,1024]{1,0:T(8,128)} async-done(((f32[192,1024]{1,0:T(8,128)}), f32[192,1024]{1,0:T(8,128)}) %all-reduce.18.cloned.1.call-update) | async-done | bytes 786448
  1074.3 1.0 multiply_reduce_fusion
  1075.2 12.4 psum.46
  1087.7 0.1 fusion.45
  1087.8 175.8 %all-gather.2 = bf16[64,3,1024]{2,1,0:T(4,128)(2,1)} all-gather(bf16[1,3,1024]{2,1,0:T(4,128)(2,1)S(1)} %fusion.45), channel_id=1, replica_groups=mesh['attn'=16,'ffn'=4,'tp'=8] {'attn','ffn'}, dimensions={0}, use_global_device_ids=true | all-gather | bytes 399360 | tf_op jit(solution)/shard_map/all_gather | solution.py:61
  1263.6 1.4 reshape.274
  1265.0 1.3 convolution_convert_fusion
  1266.3 0.0 all-reduce.14.cloned.1.call-update
  1266.3 0.0 all-reduce.20.cloned.1.call-start
  1266.4 67.9 %all-reduce.14.cloned.1.call-done = bf16[192,1024]{1,0:T(8,128)(2,1)} async-done(((bf16[192,1024]{1,0:T(8,128)(2,1)}), bf16[192,1024]{1,0:T(8,128)(2,1)}) %all-reduce.14.cloned.1.call-update) | async-done | bytes 393232 | tf_op jit(solution)/shard_map/psum | solution.py:65
  1334.3 1.1 convert_element_type.103
  1335.4 1.3 fusion.26
  1336.7 0.0 all-reduce.20.cloned.1.call-update
  1336.7 268.5 %all-reduce.20.cloned.1.call-done = f32[192,1024]{1,0:T(8,128)} async-done(((f32[192,1024]{1,0:T(8,128)}), f32[192,1024]{1,0:T(8,128)}) %all-reduce.20.cloned.1.call-update) | async-done | bytes 786448
  1605.2 0.9 fusion.46
  1606.1 0.6 pad_maximum_fusion
  (43 shorter events, 0.2 us)
Async XLA Ops:
  6.5 266.9 %copy-start = (bf16[512,1024]{1,0:T(8,128)(2,1)S(1)}, bf16[512,1024]{1,0:T(8,128)(2,1)}, u32[]{:S(2)}) copy-start(bf16[512,1024]{1,0:T(8,128)(2,1)} %param.15) | copy-start | bytes 3145732
  6.5 5.5 copy-start.8
  6.5 20.5 %copy-start.14 = (bf16[1024]{0:T(1024)(128)(2,1)S(1)}, bf16[1024]{0:T(1024)(128)(2,1)}, u32[]{:S(2)}) copy-start(bf16[1024]{0:T(1024)(128)(2,1)} %param.13) | copy-start | bytes 6148
  6.5 265.8 %all-reduce.10.cloned.1.call-start = ((), (), s32[]{:S(2)}) async-start(), calls=%async_computation | async-start | bytes 786432 | tf_op jit(solution)/shard_map/psum | solution.py:65
  12.0 15.0 copy-start.4
  27.1 175.2 %copy-start.9 = (f32[1024]{0:T(1024)}, f32[1024]{0:T(1024)S(1)}, u32[]{:S(2)}) copy-start(f32[1024]{0:T(1024)S(1)} %convert_element_type.84) | copy-start | bytes 12292
  203.6 339.7 %all-reduce.16.cloned.1.call-start = ((), (), s32[]{:S(2)}) async-start(), calls=%async_computation.3 | async-start | bytes 1572864
  274.7 268.6 %copy-start.5 = (f32[1,3,8,128]{3,2,1,0:T(8,128)S(1)}, f32[1,3,8,128]{3,2,1,0:T(8,128)}, u32[]{:S(2)}) copy-start(f32[1,3,8,128]{3,2,1,0:T(8,128)} %copy-done.4) | copy-start | bytes 36868
  274.7 282.0 %copy-start.10 = (f32[1024]{0:T(1024)S(1)}, f32[1024]{0:T(1024)}, u32[]{:S(2)}) copy-start(f32[1024]{0:T(1024)} %copy-done.9) | copy-start | bytes 12292
  274.7 528.7 %all-reduce.12.cloned.1.call-start = ((), (), s32[]{:S(2)}) async-start(), calls=%async_computation.1 | async-start | bytes 786432 | tf_op jit(solution)/shard_map/psum | solution.py:65
  278.5 278.3 %copy-start.2 = (f32[1,3,8,128]{3,2,1,0:T(8,128)}, f32[1,3,8,128]{3,2,1,0:T(8,128)S(1)}, u32[]{:S(2)}) copy-start(f32[1,3,8,128]{3,2,1,0:T(8,128)S(1)} %fusion.4) | copy-start | bytes 36868
  734.1 1.4 copy-start.12
  735.4 338.9 %all-reduce.18.cloned.1.call-start = ((), (), s32[]{:S(2)}) async-start(), calls=%async_computation.4 | async-start | bytes 1572864
  804.5 2.2 copy-start.13
  804.5 2.3 copy-start.1
  805.8 268.5 %copy-start.3 = (f32[1,3,8,128]{3,2,1,0:T(8,128)S(1)}, f32[1,3,8,128]{3,2,1,0:T(8,128)}, u32[]{:S(2)}) copy-start(f32[1,3,8,128]{3,2,1,0:T(8,128)} %copy-done.2) | copy-start | bytes 36868
  805.8 281.9 %copy-start.11 = (f32[1024]{0:T(1024)S(1)}, f32[1024]{0:T(1024)}, u32[]{:S(2)}) copy-start(f32[1024]{0:T(1024)} %copy-done.9) | copy-start | bytes 12292
  805.8 528.5 %all-reduce.14.cloned.1.call-start = ((), (), s32[]{:S(2)}) async-start(), calls=%async_computation.2 | async-start | bytes 786432 | tf_op jit(solution)/shard_map/psum | solution.py:65
  808.6 279.2 %copy-start.6 = (f32[1,3,8,128]{3,2,1,0:T(8,128)}, f32[1,3,8,128]{3,2,1,0:T(8,128)S(1)}, u32[]{:S(2)}) copy-start(f32[1,3,8,128]{3,2,1,0:T(8,128)S(1)} %fusion.3) | copy-start | bytes 36868
  1266.3 338.9 %all-reduce.20.cloned.1.call-start = ((), (), s32[]{:S(2)}) async-start(), calls=%async_computation.5 | async-start | bytes 1572864
  1335.4 269.8 %copy-start.7 = (f32[1,3,8,128]{3,2,1,0:T(8,128)S(1)}, f32[1,3,8,128]{3,2,1,0:T(8,128)}, u32[]{:S(2)}) copy-start(f32[1,3,8,128]{3,2,1,0:T(8,128)} %copy-done.6) | copy-start | bytes 36868
Sparse Core Ops, SparseCore 0:
  203.7 68.5 all-reduce.9
  276.1 267.2 all-reduce.15
  735.5 67.8 all-reduce.11
  807.0 267.2 all-reduce.17
  1266.5 67.8 all-reduce.13
  1337.9 267.2 all-reduce.19
where the time goes:
time: 1620 us; the launch traced here: 1610 us
  waiting for transfers between devices  998 us (62%)
  blocking collectives  564 us (35%)
  matrix products  20.8 us (1%)
    unnamed x9, waiting for transfers between devices  796 us
    all_gather x3, blocking collectives, on_device(): lax.all_gather(normed, ('attn', 'ffn'), axis=0, tiled=True)  524 us
    psum x3, waiting for transfers between devices, on_device(): lax.psum(partial_sums.astype(jnp.bfloat16), 'tp').astype(jnp.float32)  201 us
    psum x3, blocking collectives, on_device(): squares = lax.psum(jnp.sum(hidden_in * hidden_in, axis=1), 'tp')  39.7 us
  transfers between devices with their start and end apart: 6, of which 6 were waited for; matrix products, arithmetic and copies ran while one was open for 1% of the time, Pallas kernels for 0%

commit v1 on v0

v1 whole, which is shorter than its diff:
```python
import jax
import jax.numpy as jnp
from jax import lax
from jax.sharding import Mesh, PartitionSpec as P

D = 8192
NEAR = ("x", "zb")
FAR = ("za", "zh")
TP = ("y", "c")


def swap(array, axes):
    return lax.all_to_all(array, axes, 0, 0, tiled=True)


def spread(array, axes):
    return swap(jnp.broadcast_to(array[None], (8,) + array.shape), axes)


def attention(queries, new_kv, kv_cache, lengths):
    steps, requests, heads, size = queries.shape
    cache_length = kv_cache.shape[3]
    keys = kv_cache[:, 0, 0]
    values = kv_cache[:, 0, 1]
    rows = queries.transpose(1, 0, 2, 3).reshape(requests, steps * heads, size)
    scale = size ** (-0.5)
    scores = jnp.einsum("rqd,rld->rql", rows, keys, preferred_element_type=jnp.float32) * scale
    live = jnp.arange(cache_length, dtype=jnp.int32)[None, :] < lengths[:, None]
    scores = jnp.where(live[:, None, :], scores, -1e30)
    fresh_keys = new_kv[:, :, 0, 0]
    fresh_values = new_kv[:, :, 0, 1]
    fresh = jnp.einsum("rqd,nrd->rqn", rows, fresh_keys, preferred_element_type=jnp.float32) * scale
    row_step = jnp.arange(steps * heads, dtype=jnp.int32) // heads
    seen = jnp.arange(steps, dtype=jnp.int32)[None, :] <= row_step[:, None]
    fresh = jnp.where(seen[None], fresh, -1e30)
    top = jnp.maximum(jnp.max(scores, axis=-1), jnp.max(fresh, axis=-1))[..., None]
    cache_exp = jnp.exp(scores - top)
    fresh_exp = jnp.where(seen[None], jnp.exp(fresh - top), 0.0)
    total = jnp.sum(cache_exp, axis=-1, keepdims=True) + jnp.sum(fresh_exp, axis=-1, keepdims=True)
    cache_probs = (cache_exp / total).astype(jnp.bfloat16)
    fresh_probs = (fresh_exp / total).astype(jnp.bfloat16)
    out = jnp.einsum("rql,rld->rqd", cache_probs, values, preferred_element_type=jnp.float32)
    out = out + jnp.einsum("rqn,nrd->rqd", fresh_probs, fresh_values, preferred_element_type=jnp.float32)
    return out.reshape(requests, steps, heads * size).transpose(1, 0, 2)


def on_device(x_init, queries, new_kv, kv_cache, lengths, norm_gain, w_gate_up, w_down):
    requests, width = x_init.shape
    steps = queries.shape[0]
    units = w_gate_up.shape[2]
    w_flat = w_gate_up.reshape(width, 2 * units)
    block = 8 * requests
    with jax.named_scope("attention"):
        attended = attention(queries, new_kv, kv_cache, lengths)
    gain = norm_gain.astype(jnp.float32)
    inverse_gain = 1.0 / gain
    far_index = lax.axis_index(FAR)
    own = attended.at[0].add(x_init.astype(jnp.float32)).astype(jnp.bfloat16)
    with jax.named_scope("start_far_gather"):
        blocks = spread(own, FAR)
    blocks = blocks.astype(jnp.float32).reshape(8, steps, requests, width).transpose(1, 0, 2, 3)
    blocks = blocks.reshape(steps, block, width)
    hidden_in = blocks[0]
    results = []
    for step in range(steps):
        with jax.named_scope("near_gather"):
            rows = spread((hidden_in * gain).astype(jnp.bfloat16), NEAR).reshape(8 * block, width)
        with jax.named_scope("gate_up"):
            product = jnp.dot(rows, w_flat, preferred_element_type=jnp.float32).astype(jnp.bfloat16)
            plain = rows.astype(jnp.float32) * inverse_gain
            squares = jnp.sum(plain * plain, axis=1, keepdims=True)
            high = squares.astype(jnp.bfloat16)
            low = (squares - high.astype(jnp.float32)).astype(jnp.bfloat16)
            lane = jnp.arange(128, dtype=jnp.int32)[None, :]
            extra = jnp.where(lane == 0, high, jnp.where(lane == 1, low, jnp.zeros_like(low)))
            packed = jnp.concatenate([product, extra], axis=1).reshape(8, block, 2 * units + 128)
        with jax.named_scope("tp_scatter"):
            packed = swap(packed, TP)
        with jax.named_scope("swiglu"):
            summed = jnp.sum(packed.astype(jnp.float32), axis=0)
            mean = jnp.sum(summed[:, 2 * units :], axis=1, keepdims=True) / D
            scaled = summed[:, : 2 * units] * lax.rsqrt(mean + 1e-5)
            hidden = (jax.nn.silu(scaled[:, :units]) * scaled[:, units:]).astype(jnp.bfloat16)
        with jax.named_scope("tp_gather"):
            hidden = spread(hidden, TP).reshape(8 * block, units)
        with jax.named_scope("down"):
            down = jnp.dot(hidden, w_down, preferred_element_type=jnp.float32).astype(jnp.bfloat16)
        with jax.named_scope("near_scatter"):
            down = swap(down.reshape(8, block, width), NEAR)
        down = jnp.sum(down.astype(jnp.float32), axis=0).astype(jnp.bfloat16)
        if step + 1 < steps:
            with jax.named_scope("far_exchange"):
                down = spread(down, FAR)
            down = jnp.sum(down.astype(jnp.float32), axis=0)
            state = (hidden_in + down).astype(jnp.bfloat16)
            results.append(lax.dynamic_slice_in_dim(state, far_index * requests, requests, 0))
            hidden_in = state.astype(jnp.float32) + blocks[step + 1]
        else:
            with jax.named_scope("far_scatter"):
                down = swap(down.reshape(8, requests, width), FAR)
            down = jnp.sum(down.astype(jnp.float32), axis=0)
            mine = lax.dynamic_slice_in_dim(hidden_in, far_index * requests, requests, 0)
            results.append((mine + down).astype(jnp.bfloat16))
    return jnp.stack(results)


def solution(mesh):
    fine = Mesh(mesh.devices.reshape(4, 2, 2, 4, 4, 2), ("x", "za", "zb", "zh", "y", "c"))
    owners = ("x", "za", "zb", "zh")
    return jax.shard_map(
        on_device,
        mesh=fine,
        in_specs=(
            P(owners, TP),
            P(None, owners, TP, None),
            P(None, owners, TP, None, None),
            P(owners, TP, None, None, None),
            P(owners),
            P(TP),
            P(TP, None, owners),
            P(owners, TP),
        ),
        out_specs=P(None, owners, TP),
        check_vma=False,
    )
```

time: 1620 us -> 272 us (0.17)
  waiting for transfers between devices: 998 us -> 77.5 us
  blocking collectives: 564 us -> 114 us
  starting transfers between devices: 0.21 us -> 42.8 us
    unnamed x9 -> x0, waiting for transfers between devices: 796 us -> none
    all_gather x3 -> x0, blocking collectives: 524 us -> none  [on_device(): lax.all_gather(normed, ('attn', 'ffn'), axis=0, tiled=True)]
    psum x3 -> x0, waiting for transfers between devices: 201 us -> none  [on_device(): lax.psum(partial_sums.astype(jnp.bfloat16), 'tp').astype(jnp.float32)]
    all_to_all x0 -> x10, blocking collectives: none -> 114 us  [swap(): return lax.all_to_all(array, axes, 0, 0, tiled=True)]
    all_to_all x0 -> x6, waiting for transfers between devices: none -> 77.5 us  [swap(): return lax.all_to_all(array, axes, 0, 0, tiled=True)]
    all_to_all x0 -> x6, starting transfers between devices: none -> 42.8 us  [swap(): return lax.all_to_all(array, axes, 0, 0, tiled=True)]
    psum x3 -> x0, blocking collectives: 39.7 us -> none  [on_device(): squares = lax.psum(jnp.sum(hidden_in * hidden_in, axis=1), 'tp')]
  transfers between devices with their start and end apart: 6 -> 6, of which waited for: 6 -> 6; matrix products, arithmetic and copies ran while one was open for 1% -> 3% of each run, Pallas kernels for 0% -> 0%
where the time goes in v1:
time: 272 us; the launch traced here: 270 us
  blocking collectives  114 us (42%)
  waiting for transfers between devices  77.5 us (28%)
  starting transfers between devices  42.8 us (16%)
  local copies, waits for them, and re-layouts  15.5 us (6%)
  other arithmetic  12 us (4%)
  matrix products  7.91 us (3%)
    all_to_all x10, blocking collectives, swap(): return lax.all_to_all(array, axes, 0, 0, tiled=True)  114 us
    all_to_all x6, waiting for transfers between devices, swap(): return lax.all_to_all(array, axes, 0, 0, tiled=True)  77.5 us
    all_to_all x6, starting transfers between devices, swap(): return lax.all_to_all(array, axes, 0, 0, tiled=True)  42.8 us
  transfers between devices with their start and end apart: 6, of which 6 were waited for; matrix products, arithmetic and copies ran while one was open for 3% of the time, Pallas kernels for 0%

profile of v1, /device:TPU:32, one launch (start us, length us, event | category | flops | bytes accessed | tf_op | source)
XLA Modules:
  0.0 270.3 jit_solution(3264861771738775357)
XLA Ops:
  0.0 0.8 iota_compare_fusion
  0.8 0.8 fusion.27
  1.6 1.8 fusion.28
  3.4 0.9 fusion.29
  4.3 0.2 fusion.7
  4.5 1.4 fusion.2
  6.0 0.2 convolution_add_fusion
  6.3 0.1 scatter-add.4
  6.4 0.7 broadcast_in_dim.202
  7.2 14.2 %all-to-all-start = ((bf16[8,3,3,1024]{3,2,1,0:T(4,128)(2,1)}), bf16[8,3,3,1024]{3,2,1,0:T(4,128)(2,1)S(1)}, u32[]{:S(2)}, u32[]{:S(2)}) async-start(bf16[8,3,3,1024]{3,2,1,0:T(4,128)(2,1)} %broadcast_in_dim.202), calls=%async_computation | async-start | bytes 393216 | tf_op jit(solution)/shard_map/start_far_gather/all_to_all | solution.py:13
  21.4 17.4 %all-to-all-done = bf16[8,3,3,1024]{3,2,1,0:T(4,128)(2,1)S(1)} async-done(((bf16[8,3,3,1024]{3,2,1,0:T(4,128)(2,1)}), bf16[8,3,3,1024]{3,2,1,0:T(4,128)(2,1)S(1)}, u32[]{:S(2)}, u32[]{:S(2)}) %all-to-all-start) | async-done | bytes 147488 | tf_op jit(solution)/shard_map/start_far_gather/all_to_all | solution.py:13
  38.8 0.8 fusion.26
  39.6 0.8 broadcast_in_dim.203
  40.4 5.8 %all-to-all-start.1 = ((bf16[8,24,1024]{2,1,0:T(8,128)(2,1)}), bf16[8,24,1024]{2,1,0:T(8,128)(2,1)S(1)}, u32[]{:S(2)}, u32[]{:S(2)}) async-start(bf16[8,24,1024]{2,1,0:T(8,128)(2,1)} %broadcast_in_dim.203), calls=%async_computation.1 | async-start | bytes 786432 | tf_op jit(solution)/shard_map/near_gather/all_to_all | solution.py:13
  46.2 2.1 copy.45
  48.3 0.6 iota_compare_fusion.2
  48.9 4.1 %all-to-all-done.1 = bf16[8,24,1024]{2,1,0:T(8,128)(2,1)S(1)} async-done(((bf16[8,24,1024]{2,1,0:T(8,128)(2,1)}), bf16[8,24,1024]{2,1,0:T(8,128)(2,1)S(1)}, u32[]{:S(2)}, u32[]{:S(2)}) %all-to-all-start.1) | async-done | bytes 393248 | tf_op jit(solution)/shard_map/near_gather/all_to_all | solution.py:13
  53.0 0.2 multiply_reduce_fusion.2
  53.2 0.6 reduce_sum.171
  53.8 0.8 subtract_convert_fusion.2
  54.6 0.6 convolution_convert_fusion.5
  55.2 0.1 select_select_fusion.2
  55.3 13.8 %all_to_all.80 = bf16[8,24,1152]{2,1,0:T(8,128)(2,1)S(1)} all-to-all(bf16[8,24,1152]{2,1,0:T(8,128)(2,1)S(1)} %bitcast.87), channel_id=1, replica_groups=mesh['x'=4,'za'=2,'zb'=2,'zh'=4,'y'=4,'c'=2] {'y','c'}, dimensions={0} | all-to-all | bytes 884736 | tf_op jit(solution)/shard_map/tp_scatter/all_to_all | solution.py:13
  69.4 9.2 %all_to_all.81 = bf16[8,24,512]{2,1,0:T(8,128)(2,1)S(1)} all-to-all(bf16[8,24,512]{2,1,0:T(8,128)(2,1)S(1)} %broadcast_in_dim.209), channel_id=1, replica_groups=mesh['x'=4,'za'=2,'zb'=2,'zh'=4,'y'=4,'c'=2] {'y','c'}, dimensions={0} | all-to-all | bytes 393216 | tf_op jit(solution)/shard_map/tp_gather/all_to_all | solution.py:13
  78.7 0.4 convolution_convert_fusion.4
  79.1 11.1 %all_to_all.82 = bf16[8,24,1024]{2,1,0:T(8,128)(2,1)S(1)} all-to-all(bf16[8,24,1024]{2,1,0:T(8,128)(2,1)S(1)} %bitcast.90), channel_id=1, replica_groups=mesh['x'=4,'za'=2,'zb'=2,'zh'=4,'y'=4,'c'=2] {'x','zb'}, dimensions={0} | all-to-all | bytes 786432 | tf_op jit(solution)/shard_map/near_scatter/all_to_all | solution.py:13
  90.1 0.7 reduce_sum.174
  90.8 1.6 broadcast_in_dim.210
  92.4 4.8 %all-to-all-start.5 = ((bf16[8,24,1024]{2,1,0:T(8,128)(2,1)}), bf16[8,24,1024]{2,1,0:T(8,128)(2,1)S(1)}, u32[]{:S(2)}, u32[]{:S(2)}) async-start(bf16[8,24,1024]{2,1,0:T(8,128)(2,1)} %broadcast_in_dim.210), calls=%async_computation.5 | async-start | bytes 786432 | tf_op jit(solution)/shard_map/far_exchange/all_to_all | solution.py:13
  97.2 1.6 squeeze.26
  98.8 18.2 %all-to-all-done.5 = bf16[8,24,1024]{2,1,0:T(8,128)(2,1)S(1)} async-done(((bf16[8,24,1024]{2,1,0:T(8,128)(2,1)}), bf16[8,24,1024]{2,1,0:T(8,128)(2,1)S(1)}, u32[]{:S(2)}, u32[]{:S(2)}) %all-to-all-start.5) | async-done | bytes 393248 | tf_op jit(solution)/shard_map/far_exchange/all_to_all | solution.py:13
  117.0 1.6 multiply_convert_fusion.1
  118.6 13.4 %all_to_all.83 = bf16[8,24,1024]{2,1,0:T(8,128)(2,1)S(1)} all-to-all(bf16[8,24,1024]{2,1,0:T(8,128)(2,1)S(1)} %broadcast_in_dim.211), channel_id=1, replica_groups=mesh['x'=4,'za'=2,'zb'=2,'zh'=4,'y'=4,'c'=2] {'x','zb'}, dimensions={0} | all-to-all | bytes 786432 | tf_op jit(solution)/shard_map/near_gather/all_to_all | solution.py:13
  132.1 0.2 multiply_reduce_fusion.1
  132.2 0.6 reduce_sum.177
  132.9 0.8 subtract_convert_fusion.1
  133.7 0.6 convolution_convert_fusion.3
  134.2 0.8 select_select_fusion.1
  135.1 11.9 %all_to_all.84 = bf16[8,24,1152]{2,1,0:T(8,128)(2,1)S(1)} all-to-all(bf16[8,24,1152]{2,1,0:T(8,128)(2,1)S(1)} %bitcast.88), channel_id=1, replica_groups=mesh['x'=4,'za'=2,'zb'=2,'zh'=4,'y'=4,'c'=2] {'y','c'}, dimensions={0} | all-to-all | bytes 884736 | tf_op jit(solution)/shard_map/tp_scatter/all_to_all | solution.py:13
  147.3 9.2 %all_to_all.85 = bf16[8,24,512]{2,1,0:T(8,128)(2,1)S(1)} all-to-all(bf16[8,24,512]{2,1,0:T(8,128)(2,1)S(1)} %broadcast_in_dim.214), channel_id=1, replica_groups=mesh['x'=4,'za'=2,'zb'=2,'zh'=4,'y'=4,'c'=2] {'y','c'}, dimensions={0} | all-to-all | bytes 393216 | tf_op jit(solution)/shard_map/tp_gather/all_to_all | solution.py:13
  156.5 0.4 convolution_convert_fusion.2
  156.9 11.2 %all_to_all.86 = bf16[8,24,1024]{2,1,0:T(8,128)(2,1)S(1)} all-to-all(bf16[8,24,1024]{2,1,0:T(8,128)(2,1)S(1)} %bitcast.91), channel_id=1, replica_groups=mesh['x'=4,'za'=2,'zb'=2,'zh'=4,'y'=4,'c'=2] {'x','zb'}, dimensions={0} | all-to-all | bytes 786432 | tf_op jit(solution)/shard_map/near_scatter/all_to_all | solution.py:13
  168.1 0.7 reduce_sum.180
  168.8 1.6 broadcast_in_dim.215
  170.3 6.6 %all-to-all-start.10 = ((bf16[8,24,1024]{2,1,0:T(8,128)(2,1)}), bf16[8,24,1024]{2,1,0:T(8,128)(2,1)S(1)}, u32[]{:S(2)}, u32[]{:S(2)}) async-start(bf16[8,24,1024]{2,1,0:T(8,128)(2,1)} %broadcast_in_dim.215), calls=%async_computation.10 | async-start | bytes 786432 | tf_op jit(solution)/shard_map/far_exchange/all_to_all | solution.py:13
  177.0 1.6 squeeze.27
  178.6 18.2 %all-to-all-done.10 = bf16[8,24,1024]{2,1,0:T(8,128)(2,1)S(1)} async-done(((bf16[8,24,1024]{2,1,0:T(8,128)(2,1)}), bf16[8,24,1024]{2,1,0:T(8,128)(2,1)S(1)}, u32[]{:S(2)}, u32[]{:S(2)}) %all-to-all-start.10) | async-done | bytes 393248 | tf_op jit(solution)/shard_map/far_exchange/all_to_all | solution.py:13
  196.8 1.6 multiply_convert_fusion
  198.5 13.3 %all_to_all.87 = bf16[8,24,1024]{2,1,0:T(8,128)(2,1)S(1)} all-to-all(bf16[8,24,1024]{2,1,0:T(8,128)(2,1)S(1)} %broadcast_in_dim.216), channel_id=1, replica_groups=mesh['x'=4,'za'=2,'zb'=2,'zh'=4,'y'=4,'c'=2] {'x','zb'}, dimensions={0} | all-to-all | bytes 786432 | tf_op jit(solution)/shard_map/near_gather/all_to_all | solution.py:13
  211.8 0.2 multiply_reduce_fusion
  212.1 0.6 convolution_convert_fusion.1
  212.7 0.1 select_select_fusion
  212.9 11.9 %all_to_all.88 = bf16[8,24,1152]{2,1,0:T(8,128)(2,1)S(1)} all-to-all(bf16[8,24,1152]{2,1,0:T(8,128)(2,1)S(1)} %bitcast.89), channel_id=1, replica_groups=mesh['x'=4,'za'=2,'zb'=2,'zh'=4,'y'=4,'c'=2] {'y','c'}, dimensions={0} | all-to-all | bytes 884736 | tf_op jit(solution)/shard_map/tp_scatter/all_to_all | solution.py:13
  225.1 9.2 %all_to_all.89 = bf16[8,24,512]{2,1,0:T(8,128)(2,1)S(1)} all-to-all(bf16[8,24,512]{2,1,0:T(8,128)(2,1)S(1)} %broadcast_in_dim.219), channel_id=1, replica_groups=mesh['x'=4,'za'=2,'zb'=2,'zh'=4,'y'=4,'c'=2] {'y','c'}, dimensions={0} | all-to-all | bytes 393216 | tf_op jit(solution)/shard_map/tp_gather/all_to_all | solution.py:13
  234.3 1.1 convolution_convert_fusion
  235.5 4.6 %all-to-all-start.14 = ((bf16[8,24,1024]{2,1,0:T(8,128)(2,1)}), bf16[8,24,1024]{2,1,0:T(8,128)(2,1)S(1)}, u32[]{:S(2)}, u32[]{:S(2)}) async-start(bf16[8,24,1024]{2,1,0:T(8,128)(2,1)} %bitcast.24), calls=%async_computation.14 | async-start | bytes 786432 | tf_op jit(solution)/shard_map/near_scatter/all_to_all | solution.py:13
  240.1 7.5 %all-to-all-done.14 = bf16[8,24,1024]{2,1,0:T(8,128)(2,1)S(1)} async-done(((bf16[8,24,1024]{2,1,0:T(8,128)(2,1)}), bf16[8,24,1024]{2,1,0:T(8,128)(2,1)S(1)}, u32[]{:S(2)}, u32[]{:S(2)}) %all-to-all-start.14) | async-done | bytes 393248 | tf_op jit(solution)/shard_map/near_scatter/all_to_all | solution.py:13
  247.7 0.7 reshape.367
  248.4 6.7 %all-to-all-start.15 = ((bf16[8,3,1024]{2,1,0:T(4,128)(2,1)}), bf16[8,3,1024]{2,1,0:T(4,128)(2,1)S(1)}, u32[]{:S(2)}, u32[]{:S(2)}) async-start(bf16[8,3,1024]{2,1,0:T(4,128)(2,1)} %reshape.367), calls=%async_computation.15 | async-start | bytes 131072 | tf_op jit(solution)/shard_map/far_scatter/all_to_all | solution.py:13
  255.1 0.8 dynamic-slice_bitcast_fusion.1
  255.9 0.8 dynamic-slice_bitcast_fusion
  256.6 12.1 %all-to-all-done.15 = bf16[8,3,1024]{2,1,0:T(4,128)(2,1)S(1)} async-done(((bf16[8,3,1024]{2,1,0:T(4,128)(2,1)}), bf16[8,3,1024]{2,1,0:T(4,128)(2,1)S(1)}, u32[]{:S(2)}, u32[]{:S(2)}) %all-to-all-start.15) | async-done | bytes 49184 | tf_op jit(solution)/shard_map/far_scatter/all_to_all | solution.py:13
  268.8 0.9 fusion.19
  269.6 0.6 pad_maximum_fusion.3
  (57 shorter events, 1.6 us)
Async XLA Ops:
  0.0 78.7 %copy-start = (bf16[512,1024]{1,0:T(8,128)(2,1)S(1)}, bf16[512,1024]{1,0:T(8,128)(2,1)}, u32[]{:S(2)}) copy-start(bf16[512,1024]{1,0:T(8,128)(2,1)} %param.17) | copy-start | bytes 3145732
  0.0 6.2 %copy-start.3 = (bf16[3,1024]{1,0:T(4,128)(2,1)S(1)}, bf16[3,1024]{1,0:T(4,128)(2,1)}, u32[]{:S(2)}) copy-start(bf16[3,1024]{1,0:T(4,128)(2,1)} %param.10) | copy-start | bytes 18436
  1.6 19.7 %copy-start.2 = (bf16[1024]{0:T(1024)(128)(2,1)S(1)}, bf16[1024]{0:T(1024)(128)(2,1)}, u32[]{:S(2)}) copy-start(bf16[1024]{0:T(1024)(128)(2,1)} %param.15) | copy-start | bytes 6148
  7.2 31.6 %all-to-all-start = ((bf16[8,3,3,1024]{3,2,1,0:T(4,128)(2,1)}), bf16[8,3,3,1024]{3,2,1,0:T(4,128)(2,1)S(1)}, u32[]{:S(2)}, u32[]{:S(2)}) async-start(bf16[8,3,3,1024]{3,2,1,0:T(4,128)(2,1)} %broadcast_in_dim.202), calls=%async_computation | async-start | bytes 393216 | tf_op jit(solution)/shard_map/start_far_gather/all_to_all | solution.py:13
  39.6 6.6 %copy-start.1 = (f32[24,1024]{1,0:T(8,128)}, f32[24,1024]{1,0:T(8,128)S(1)}, u32[]{:S(2)}) copy-start(f32[24,1024]{1,0:T(8,128)S(1)} %squeeze.25) | copy-start | bytes 294916
  40.4 12.6 %all-to-all-start.1 = ((bf16[8,24,1024]{2,1,0:T(8,128)(2,1)}), bf16[8,24,1024]{2,1,0:T(8,128)(2,1)S(1)}, u32[]{:S(2)}, u32[]{:S(2)}) async-start(bf16[8,24,1024]{2,1,0:T(8,128)(2,1)} %broadcast_in_dim.203), calls=%async_computation.1 | async-start | bytes 786432 | tf_op jit(solution)/shard_map/near_gather/all_to_all | solution.py:13
  53.8 1.3 copy-start.4
  92.4 24.6 %all-to-all-start.5 = ((bf16[8,24,1024]{2,1,0:T(8,128)(2,1)}), bf16[8,24,1024]{2,1,0:T(8,128)(2,1)S(1)}, u32[]{:S(2)}, u32[]{:S(2)}) async-start(bf16[8,24,1024]{2,1,0:T(8,128)(2,1)} %broadcast_in_dim.210), calls=%async_computation.5 | async-start | bytes 786432 | tf_op jit(solution)/shard_map/far_exchange/all_to_all | solution.py:13
  170.3 26.4 %all-to-all-start.10 = ((bf16[8,24,1024]{2,1,0:T(8,128)(2,1)}), bf16[8,24,1024]{2,1,0:T(8,128)(2,1)S(1)}, u32[]{:S(2)}, u32[]{:S(2)}) async-start(bf16[8,24,1024]{2,1,0:T(8,128)(2,1)} %broadcast_in_dim.215), calls=%async_computation.10 | async-start | bytes 786432 | tf_op jit(solution)/shard_map/far_exchange/all_to_all | solution.py:13
  198.5 14.2 %copy-start.5 = (pred[128]{0:T(512)(128)(4,1)S(1)}, pred[128]{0:T(512)(128)(4,1)}, u32[]{:S(2)}) copy-start(pred[128]{0:T(512)(128)(4,1)} %get-tuple-element.38) | copy-start | bytes 388
  235.5 12.2 %all-to-all-start.14 = ((bf16[8,24,1024]{2,1,0:T(8,128)(2,1)}), bf16[8,24,1024]{2,1,0:T(8,128)(2,1)S(1)}, u32[]{:S(2)}, u32[]{:S(2)}) async-start(bf16[8,24,1024]{2,1,0:T(8,128)(2,1)} %bitcast.24), calls=%async_computation.14 | async-start | bytes 786432 | tf_op jit(solution)/shard_map/near_scatter/all_to_all | solution.py:13
  248.4 20.4 %all-to-all-start.15 = ((bf16[8,3,1024]{2,1,0:T(4,128)(2,1)}), bf16[8,3,1024]{2,1,0:T(4,128)(2,1)S(1)}, u32[]{:S(2)}, u32[]{:S(2)}) async-start(bf16[8,3,1024]{2,1,0:T(4,128)(2,1)} %reshape.367), calls=%async_computation.15 | async-start | bytes 131072 | tf_op jit(solution)/shard_map/far_scatter/all_to_all | solution.py:13

commit v2 on v1

--- a/solution.py
+++ b/solution.py
@@ -44,63 +44,111 @@
     return out.reshape(requests, steps, heads * size).transpose(1, 0, 2)
 
 
+def place_rows(mine, far_index):
+    count, width = mine.shape
+    row_far = jnp.arange(8, dtype=jnp.int32)[None, :, None]
+    return jnp.where(row_far == far_index, mine[:, None, :], 0.0).reshape(8 * count, width)
+
+
+def own_rows(rows, far_index):
+    count = rows.shape[-2] // 8
+    split = rows.reshape(rows.shape[:-2] + (count, 8, rows.shape[-1]))
+    taken = lax.dynamic_slice_in_dim(split, far_index, 1, split.ndim - 2)
+    return taken.reshape(rows.shape[:-2] + (count, rows.shape[-1]))
+
+
 def on_device(x_init, queries, new_kv, kv_cache, lengths, norm_gain, w_gate_up, w_down):
     requests, width = x_init.shape
     steps = queries.shape[0]
     units = w_gate_up.shape[2]
     w_flat = w_gate_up.reshape(width, 2 * units)
-    block = 8 * requests
     with jax.named_scope("attention"):
         attended = attention(queries, new_kv, kv_cache, lengths)
     gain = norm_gain.astype(jnp.float32)
     inverse_gain = 1.0 / gain
     far_index = lax.axis_index(FAR)
-    own = attended.at[0].add(x_init.astype(jnp.float32)).astype(jnp.bfloat16)
+    own_first = x_init.astype(jnp.float32) + attended[0]
     with jax.named_scope("start_far_gather"):
-        blocks = spread(own, FAR)
-    blocks = blocks.astype(jnp.float32).reshape(8, steps, requests, width).transpose(1, 0, 2, 3)
-    blocks = blocks.reshape(steps, block, width)
-    hidden_in = blocks[0]
-    results = []
-    for step in range(steps):
+        blocks = spread(own_first.astype(jnp.bfloat16), FAR)
+    blocks, w_flat = lax.optimization_barrier((blocks, w_flat))
+    blocks = blocks.astype(jnp.float32).transpose(1, 0, 2)
+
+    def near_gather(hidden_in):
         with jax.named_scope("near_gather"):
-            rows = spread((hidden_in * gain).astype(jnp.bfloat16), NEAR).reshape(8 * block, width)
+            return spread((hidden_in * gain).astype(jnp.bfloat16), NEAR)
+
+    def gate_up(rows):
+        block = rows.shape[1]
         with jax.named_scope("gate_up"):
-            product = jnp.dot(rows, w_flat, preferred_element_type=jnp.float32).astype(jnp.bfloat16)
+            product = jnp.dot(
+                rows.reshape(8 * block, width), w_flat, preferred_element_type=jnp.float32
+            ).astype(jnp.bfloat16)
             plain = rows.astype(jnp.float32) * inverse_gain
-            squares = jnp.sum(plain * plain, axis=1, keepdims=True)
-            high = squares.astype(jnp.bfloat16)
-            low = (squares - high.astype(jnp.float32)).astype(jnp.bfloat16)
-            lane = jnp.arange(128, dtype=jnp.int32)[None, :]
-            extra = jnp.where(lane == 0, high, jnp.where(lane == 1, low, jnp.zeros_like(low)))
-            packed = jnp.concatenate([product, extra], axis=1).reshape(8, block, 2 * units + 128)
+            squares = plain * plain
+            folded = squares[..., :128]
+            for lane in range(128, width, 128):
+                folded = folded + squares[..., lane : lane + 128]
+            packed = jnp.concatenate(
+                [product.reshape(8, block, 2 * units), folded.astype(jnp.bfloat16)], axis=2
+            )
         with jax.named_scope("tp_scatter"):
-            packed = swap(packed, TP)
+            return swap(packed, TP)
+
+    def swiglu(packed):
         with jax.named_scope("swiglu"):
             summed = jnp.sum(packed.astype(jnp.float32), axis=0)
             mean = jnp.sum(summed[:, 2 * units :], axis=1, keepdims=True) / D
             scaled = summed[:, : 2 * units] * lax.rsqrt(mean + 1e-5)
             hidden = (jax.nn.silu(scaled[:, :units]) * scaled[:, units:]).astype(jnp.bfloat16)
         with jax.named_scope("tp_gather"):
-            hidden = spread(hidden, TP).reshape(8 * block, units)
+            return spread(hidden, TP)
+
+    def down_product(hidden):
+        block = hidden.shape[1]
         with jax.named_scope("down"):
-            down = jnp.dot(hidden, w_down, preferred_element_type=jnp.float32).astype(jnp.bfloat16)
+            down = jnp.dot(
+                hidden.reshape(8 * block, units), w_down, preferred_element_type=jnp.float32
+            ).astype(jnp.bfloat16)
         with jax.named_scope("near_scatter"):
-            down = swap(down.reshape(8, block, width), NEAR)
-        down = jnp.sum(down.astype(jnp.float32), axis=0).astype(jnp.bfloat16)
+            return swap(down.reshape(8, block, width), NEAR)
+
+    def far_exchange(down, coming):
+        near_sum = jnp.sum(down.astype(jnp.float32), axis=0)
+        sent = (near_sum + place_rows(coming, far_index)).astype(jnp.bfloat16)
+        with jax.named_scope("far_exchange"):
+            return near_sum, sent, spread(sent, FAR)
+
+    def far_scatter(down):
+        near_sum = jnp.sum(down.astype(jnp.float32), axis=0).astype(jnp.bfloat16)
+        count = near_sum.shape[0] // 8
+        with jax.named_scope("far_scatter"):
+            return swap(near_sum.reshape(count, 8, width).transpose(1, 0, 2), FAR)
+
+    chains = ((0, 3),)
+    hidden_in = [blocks[a:b].reshape((b - a) * 8, width) for a, b in chains]
+    own_hidden = [own_first[a:b] for a, b in chains]
+    results = []
+    for step in range(steps):
+        data = [near_gather(h) for h in hidden_in]
+        data = [gate_up(d) for d in data]
+        data = [swiglu(d) for d in data]
+        data = [down_product(d) for d in data]
         if step + 1 < steps:
-            with jax.named_scope("far_exchange"):
-                down = spread(down, FAR)
-            down = jnp.sum(down.astype(jnp.float32), axis=0)
-            state = (hidden_in + down).astype(jnp.bfloat16)
-            results.append(lax.dynamic_slice_in_dim(state, far_index * requests, requests, 0))
-            hidden_in = state.astype(jnp.float32) + blocks[step + 1]
+            coming = [attended[step + 1, a:b] for a, b in chains]
+            data = [far_exchange(d, c) for d, c in zip(data, coming)]
+            hidden_in = [h + jnp.sum(d[2].astype(jnp.float32), axis=0) for h, d in zip(hidden_in, data)]
+            own_down = [
+                jnp.sum(own_rows(got, far_index).astype(jnp.float32), axis=0)
+                - own_rows(sent, far_index).astype(jnp.float32)
+                + own_rows(near_sum, far_index)
+                for near_sum, sent, got in data
+            ]
         else:
-            with jax.named_scope("far_scatter"):
-                down = swap(down.reshape(8, requests, width), FAR)
-            down = jnp.sum(down.astype(jnp.float32), axis=0)
-            mine = lax.dynamic_slice_in_dim(hidden_in, far_index * requests, requests, 0)
-            results.append((mine + down).astype(jnp.bfloat16))
+            own_down = [jnp.sum(far_scatter(d).astype(jnp.float32), axis=0) for d in data]
+        state = [(h + d).astype(jnp.bfloat16) for h, d in zip(own_hidden, own_down)]
+        results.append(jnp.concatenate(state, axis=0))
+        if step + 1 < steps:
+            own_hidden = [s.astype(jnp.float32) + c for s, c in zip(state, coming)]
     return jnp.stack(results)
 
 

time: 272 us -> 258 us (0.949)
  blocking collectives: 114 us -> 155 us
  waiting for transfers between devices: 77.5 us -> 40.3 us
  starting transfers between devices: 42.8 us -> 33.5 us
  other arithmetic: 12 us -> 5.23 us
    all_to_all x10 -> x11, blocking collectives: 114 us -> 155 us  [swap(): return lax.all_to_all(array, axes, 0, 0, tiled=True)]
    all_to_all x6 -> x5, waiting for transfers between devices: 77.5 us -> 40.3 us  [swap(): return lax.all_to_all(array, axes, 0, 0, tiled=True)]
    all_to_all x6 -> x5, starting transfers between devices: 42.8 us -> 33.5 us  [swap(): return lax.all_to_all(array, axes, 0, 0, tiled=True)]
    dynamic_slice x0 -> x5, local copies, waits for them, and re-layouts: none -> 3.68 us  [own_rows(): taken = lax.dynamic_slice_in_dim(split, far_index, 1, split.ndim - 2)]
    convert_element_type x10 -> x12, other arithmetic: 4.85 us -> 1.22 us  [the longest x2 0.89 us: far_exchange(): sent = (near_sum + place_rows(coming, far_index)).astype(jnp.bfloat16)]
    squeeze x3 -> x0, local copies, waits for them, and re-layouts: 3.23 us -> none  [the longest x2 3.18 us: on_device(): hidden_in = state.astype(jnp.float32) + blocks[step + 1]]
    broadcast_in_dim x9, local copies, waits for them, and re-layouts: 4.77 us -> 1.59 us  [spread(): return swap(jnp.broadcast_to(array[None], (8,) + array.shape), axes)]
    unnamed x13 -> x39, local copies, waits for them, and re-layouts: 2.17 us -> 5.19 us
  transfers between devices with their start and end apart: 6 -> 5, of which waited for: 6 -> 5; matrix products, arithmetic and copies ran while one was open for 3% -> 3% of each run, Pallas kernels for 0% -> 0%
where the time goes in v2:
time: 258 us; the launch traced here: 257 us
  blocking collectives  155 us (60%)
  waiting for transfers between devices  40.3 us (16%)
  starting transfers between devices  33.5 us (13%)
  local copies, waits for them, and re-layouts  14 us (5%)
  matrix products  8.65 us (3%)
  other arithmetic  5.23 us (2%)
    all_to_all x11, blocking collectives, swap(): return lax.all_to_all(array, axes, 0, 0, tiled=True)  155 us
    all_to_all x5, waiting for transfers between devices, swap(): return lax.all_to_all(array, axes, 0, 0, tiled=True)  40.3 us
    all_to_all x5, starting transfers between devices, swap(): return lax.all_to_all(array, axes, 0, 0, tiled=True)  33.5 us
    unnamed x39, local copies, waits for them, and re-layouts  5.19 us
  transfers between devices with their start and end apart: 5, of which 5 were waited for; matrix products, arithmetic and copies ran while one was open for 3% of the time, Pallas kernels for 0%

profile of v2, /device:TPU:32, one launch (start us, length us, event | category | flops | bytes accessed | tf_op | source)
XLA Modules:
  0.0 256.8 jit_solution(9986759422681627131)
XLA Ops:
  0.0 0.8 iota_compare_fusion
  0.8 0.8 fusion.46
  1.6 0.9 fusion.48
  2.5 1.8 fusion.47
  4.3 0.2 fusion.7
  4.5 1.4 fusion.2
  5.9 0.2 convolution_add_fusion
  6.2 0.6 copy-done.6
  6.8 0.6 broadcast_in_dim.157
  7.5 14.2 %all-to-all-start = ((bf16[8,3,1024]{2,1,0:T(4,128)(2,1)}), bf16[8,3,1024]{2,1,0:T(4,128)(2,1)S(1)}, u32[]{:S(2)}, u32[]{:S(2)}) async-start(bf16[8,3,1024]{2,1,0:T(4,128)(2,1)} %broadcast_in_dim.157), calls=%async_computation | async-start | bytes 131072 | tf_op jit(solution)/shard_map/start_far_gather/all_to_all | solution.py:13
  21.7 2.1 copy.74
  23.9 11.2 %all-to-all-done = bf16[8,3,1024]{2,1,0:T(4,128)(2,1)S(1)} async-done(((bf16[8,3,1024]{2,1,0:T(4,128)(2,1)}), bf16[8,3,1024]{2,1,0:T(4,128)(2,1)S(1)}, u32[]{:S(2)}, u32[]{:S(2)}) %all-to-all-start) | async-done | bytes 49184 | tf_op jit(solution)/shard_map/start_far_gather/all_to_all | solution.py:13
  35.1 0.8 broadcast_in_dim.158
  35.9 5.8 %all-to-all-start.1 = ((bf16[8,24,1024]{2,1,0:T(8,128)(2,1)}), bf16[8,24,1024]{2,1,0:T(8,128)(2,1)S(1)}, u32[]{:S(2)}, u32[]{:S(2)}) async-start(bf16[8,24,1024]{2,1,0:T(8,128)(2,1)} %broadcast_in_dim.158), calls=%async_computation.1 | async-start | bytes 786432 | tf_op jit(solution)/shard_map/near_gather/all_to_all | solution.py:13
  41.7 6.8 %all-to-all-done.1 = bf16[8,24,1024]{2,1,0:T(8,128)(2,1)S(1)} async-done(((bf16[8,24,1024]{2,1,0:T(8,128)(2,1)}), bf16[8,24,1024]{2,1,0:T(8,128)(2,1)S(1)}, u32[]{:S(2)}, u32[]{:S(2)}) %all-to-all-start.1) | async-done | bytes 393248 | tf_op jit(solution)/shard_map/near_gather/all_to_all | solution.py:13
  48.5 0.1 multiply_multiply_fusion.2
  48.7 0.6 convolution_convert_fusion.5
  49.3 13.8 %all_to_all.80 = bf16[8,24,1152]{2,1,0:T(8,128)(2,1)S(1)} all-to-all(bf16[8,24,1152]{2,1,0:T(8,128)(2,1)S(1)} %pad_maximum_fusion), channel_id=1, replica_groups=mesh['x'=4,'za'=2,'zb'=2,'zh'=4,'y'=4,'c'=2] {'y','c'}, dimensions={0} | all-to-all | bytes 884736 | tf_op jit(solution)/shard_map/tp_scatter/all_to_all | solution.py:13
  63.1 0.1 slice_reduce_fusion.2
  63.2 0.1 slice_multiply_fusion.2
  63.4 9.2 %all_to_all.81 = bf16[8,24,512]{2,1,0:T(8,128)(2,1)S(1)} all-to-all(bf16[8,24,512]{2,1,0:T(8,128)(2,1)S(1)} %broadcast_in_dim.159), channel_id=1, replica_groups=mesh['x'=4,'za'=2,'zb'=2,'zh'=4,'y'=4,'c'=2] {'y','c'}, dimensions={0} | all-to-all | bytes 393216 | tf_op jit(solution)/shard_map/tp_gather/all_to_all | solution.py:13
  72.6 1.1 convolution_convert_fusion.4
  73.7 4.5 %all-to-all-start.4 = ((bf16[8,24,1024]{2,1,0:T(8,128)(2,1)}), bf16[8,24,1024]{2,1,0:T(8,128)(2,1)S(1)}, u32[]{:S(2)}, u32[]{:S(2)}) async-start(bf16[8,24,1024]{2,1,0:T(8,128)(2,1)} %bitcast.151), calls=%async_computation.4 | async-start | bytes 786432 | tf_op jit(solution)/shard_map/near_scatter/all_to_all | solution.py:13
  78.3 0.6 copy-done.17
  78.9 0.7 broadcast_in_dim.161
  79.5 1.3 slice_bitcast_fusion
  80.9 4.9 %all-to-all-done.4 = bf16[8,24,1024]{2,1,0:T(8,128)(2,1)S(1)} async-done(((bf16[8,24,1024]{2,1,0:T(8,128)(2,1)}), bf16[8,24,1024]{2,1,0:T(8,128)(2,1)S(1)}, u32[]{:S(2)}, u32[]{:S(2)}) %all-to-all-start.4) | async-done | bytes 393248 | tf_op jit(solution)/shard_map/near_scatter/all_to_all | solution.py:13
  85.9 0.6 copy-done.4
  86.5 0.8 fusion.17
  87.3 25.8 %all_to_all.82 = bf16[8,24,1024]{2,1,0:T(8,128)(2,1)S(1)} all-to-all(bf16[8,24,1024]{2,1,0:T(8,128)(2,1)S(1)} %broadcast_in_dim.167), channel_id=1, replica_groups=mesh['x'=4,'za'=2,'zb'=2,'zh'=4,'y'=4,'c'=2] {'za','zh'}, dimensions={0} | all-to-all | bytes 786432 | tf_op jit(solution)/shard_map/far_exchange/all_to_all | solution.py:13
  113.3 11.7 %all_to_all.83 = bf16[8,24,1024]{2,1,0:T(8,128)(2,1)S(1)} all-to-all(bf16[8,24,1024]{2,1,0:T(8,128)(2,1)S(1)} %broadcast_in_dim.170), channel_id=1, replica_groups=mesh['x'=4,'za'=2,'zb'=2,'zh'=4,'y'=4,'c'=2] {'x','zb'}, dimensions={0} | all-to-all | bytes 786432 | tf_op jit(solution)/shard_map/near_gather/all_to_all | solution.py:13
  125.0 0.6 convolution_convert_fusion.3
  125.6 0.1 multiply_multiply_fusion.1
  125.8 11.9 %all_to_all.84 = bf16[8,24,1152]{2,1,0:T(8,128)(2,1)S(1)} all-to-all(bf16[8,24,1152]{2,1,0:T(8,128)(2,1)S(1)} %pad_maximum_fusion.1), channel_id=1, replica_groups=mesh['x'=4,'za'=2,'zb'=2,'zh'=4,'y'=4,'c'=2] {'y','c'}, dimensions={0} | all-to-all | bytes 884736 | tf_op jit(solution)/shard_map/tp_scatter/all_to_all | solution.py:13
  137.7 0.1 slice_reduce_fusion.1
  137.9 0.1 slice_multiply_fusion.1
  138.0 9.2 %all_to_all.85 = bf16[8,24,512]{2,1,0:T(8,128)(2,1)S(1)} all-to-all(bf16[8,24,512]{2,1,0:T(8,128)(2,1)S(1)} %broadcast_in_dim.171), channel_id=1, replica_groups=mesh['x'=4,'za'=2,'zb'=2,'zh'=4,'y'=4,'c'=2] {'y','c'}, dimensions={0} | all-to-all | bytes 393216 | tf_op jit(solution)/shard_map/tp_gather/all_to_all | solution.py:13
  147.2 0.4 convolution_convert_fusion.2
  147.6 11.2 %all_to_all.86 = bf16[8,24,1024]{2,1,0:T(8,128)(2,1)S(1)} all-to-all(bf16[8,24,1024]{2,1,0:T(8,128)(2,1)S(1)} %bitcast.152), channel_id=1, replica_groups=mesh['x'=4,'za'=2,'zb'=2,'zh'=4,'y'=4,'c'=2] {'x','zb'}, dimensions={0} | all-to-all | bytes 786432 | tf_op jit(solution)/shard_map/near_scatter/all_to_all | solution.py:13
  158.9 0.1 fusion.14
  159.0 0.5 copy-done.5
  159.5 28.1 %all_to_all.87 = bf16[8,24,1024]{2,1,0:T(8,128)(2,1)S(1)} all-to-all(bf16[8,24,1024]{2,1,0:T(8,128)(2,1)S(1)} %broadcast_in_dim.175), channel_id=1, replica_groups=mesh['x'=4,'za'=2,'zb'=2,'zh'=4,'y'=4,'c'=2] {'za','zh'}, dimensions={0} | all-to-all | bytes 786432 | tf_op jit(solution)/shard_map/far_exchange/all_to_all | solution.py:13
  187.8 0.6 copy-done.1
  188.5 12.1 %all_to_all.88 = bf16[8,24,1024]{2,1,0:T(8,128)(2,1)S(1)} all-to-all(bf16[8,24,1024]{2,1,0:T(8,128)(2,1)S(1)} %broadcast_in_dim.176), channel_id=1, replica_groups=mesh['x'=4,'za'=2,'zb'=2,'zh'=4,'y'=4,'c'=2] {'x','zb'}, dimensions={0} | all-to-all | bytes 786432 | tf_op jit(solution)/shard_map/near_gather/all_to_all | solution.py:13
  200.6 0.6 convolution_convert_fusion.1
  201.1 0.1 multiply_multiply_fusion
  201.3 12.3 %all_to_all.89 = bf16[8,24,1152]{2,1,0:T(8,128)(2,1)S(1)} all-to-all(bf16[8,24,1152]{2,1,0:T(8,128)(2,1)S(1)} %pad_maximum_fusion.2), channel_id=1, replica_groups=mesh['x'=4,'za'=2,'zb'=2,'zh'=4,'y'=4,'c'=2] {'y','c'}, dimensions={0} | all-to-all | bytes 884736 | tf_op jit(solution)/shard_map/tp_scatter/all_to_all | solution.py:13
  213.7 0.1 slice_reduce_fusion
  213.8 0.1 slice_multiply_fusion
  214.0 9.4 %all_to_all.90 = bf16[8,24,512]{2,1,0:T(8,128)(2,1)S(1)} all-to-all(bf16[8,24,512]{2,1,0:T(8,128)(2,1)S(1)} %broadcast_in_dim.177), channel_id=1, replica_groups=mesh['x'=4,'za'=2,'zb'=2,'zh'=4,'y'=4,'c'=2] {'y','c'}, dimensions={0} | all-to-all | bytes 393216 | tf_op jit(solution)/shard_map/tp_gather/all_to_all | solution.py:13
  223.3 1.1 convolution_convert_fusion
  224.5 4.6 %all-to-all-start.14 = ((bf16[8,24,1024]{2,1,0:T(8,128)(2,1)}), bf16[8,24,1024]{2,1,0:T(8,128)(2,1)S(1)}, u32[]{:S(2)}, u32[]{:S(2)}) async-start(bf16[8,24,1024]{2,1,0:T(8,128)(2,1)} %bitcast.35), calls=%async_computation.14 | async-start | bytes 786432 | tf_op jit(solution)/shard_map/near_scatter/all_to_all | solution.py:13
  229.1 0.7 dynamic-slice
  229.8 0.9 constant_dynamic-slice_fusion.2
  230.7 0.1 constant_dynamic-slice_fusion.3
  230.8 0.9 constant_dynamic-slice_fusion.1
  231.7 4.9 %all-to-all-done.14 = bf16[8,24,1024]{2,1,0:T(8,128)(2,1)S(1)} async-done(((bf16[8,24,1024]{2,1,0:T(8,128)(2,1)}), bf16[8,24,1024]{2,1,0:T(8,128)(2,1)S(1)}, u32[]{:S(2)}, u32[]{:S(2)}) %all-to-all-start.14) | async-done | bytes 393248 | tf_op jit(solution)/shard_map/near_scatter/all_to_all | solution.py:13
  236.7 0.7 copy.59
  237.4 4.4 %all-to-all-start.15 = ((bf16[8,3,1024]{2,1,0:T(4,128)(2,1)}), bf16[8,3,1024]{2,1,0:T(4,128)(2,1)S(1)}, u32[]{:S(2)}, u32[]{:S(2)}) async-start(bf16[8,3,1024]{2,1,0:T(4,128)(2,1)} %copy.59), calls=%async_computation.15 | async-start | bytes 131072 | tf_op jit(solution)/shard_map/far_scatter/all_to_all | solution.py:13
  241.7 1.1 constant_dynamic-slice_fusion
  242.8 0.1 convert_reduce_fusion.8
  242.9 12.4 %all-to-all-done.15 = bf16[8,3,1024]{2,1,0:T(4,128)(2,1)S(1)} async-done(((bf16[8,3,1024]{2,1,0:T(4,128)(2,1)}), bf16[8,3,1024]{2,1,0:T(4,128)(2,1)S(1)}, u32[]{:S(2)}, u32[]{:S(2)}) %all-to-all-start.15) | async-done | bytes 49184 | tf_op jit(solution)/shard_map/far_scatter/all_to_all | solution.py:13
  255.4 0.7 fusion.35
  256.2 0.6 pad_maximum_fusion.3
  (76 shorter events, 1.3 us)
Async XLA Ops:
  0.0 72.6 %copy-start = (bf16[512,1024]{1,0:T(8,128)(2,1)S(1)}, bf16[512,1024]{1,0:T(8,128)(2,1)}, u32[]{:S(2)}) copy-start(bf16[512,1024]{1,0:T(8,128)(2,1)} %param.15) | copy-start | bytes 3145732
  0.0 6.8 %copy-start.13 = (bf16[3,1024]{1,0:T(4,128)(2,1)S(1)}, bf16[3,1024]{1,0:T(4,128)(2,1)}, u32[]{:S(2)}) copy-start(bf16[3,1024]{1,0:T(4,128)(2,1)} %param.8) | copy-start | bytes 18436
  0.0 21.7 %copy-start.15 = (bf16[1024]{0:T(1024)(128)(2,1)S(1)}, bf16[1024]{0:T(1024)(128)(2,1)}, u32[]{:S(2)}) copy-start(bf16[1024]{0:T(1024)(128)(2,1)} %param.13) | copy-start | bytes 6148
  6.2 0.6 copy-start.6
  7.5 27.6 %all-to-all-start = ((bf16[8,3,1024]{2,1,0:T(4,128)(2,1)}), bf16[8,3,1024]{2,1,0:T(4,128)(2,1)S(1)}, u32[]{:S(2)}, u32[]{:S(2)}) async-start(bf16[8,3,1024]{2,1,0:T(4,128)(2,1)} %broadcast_in_dim.157), calls=%async_computation | async-start | bytes 131072 | tf_op jit(solution)/shard_map/start_far_gather/all_to_all | solution.py:13
  21.7 13.4 %copy-start.11 = (f32[1024]{0:T(1024)}, f32[1024]{0:T(1024)S(1)}, u32[]{:S(2)}) copy-start(f32[1024]{0:T(1024)S(1)} %convert_element_type.167) | copy-start | bytes 12292
  35.1 0.8 copy-start.2
  35.9 12.6 %all-to-all-start.1 = ((bf16[8,24,1024]{2,1,0:T(8,128)(2,1)}), bf16[8,24,1024]{2,1,0:T(8,128)(2,1)S(1)}, u32[]{:S(2)}, u32[]{:S(2)}) async-start(bf16[8,24,1024]{2,1,0:T(8,128)(2,1)} %broadcast_in_dim.158), calls=%async_computation.1 | async-start | bytes 786432 | tf_op jit(solution)/shard_map/near_gather/all_to_all | solution.py:13
  41.7 7.6 %copy-start.9 = (f32[1024]{0:T(1024)}, f32[1024]{0:T(1024)S(1)}, u32[]{:S(2)}) copy-start(f32[1024]{0:T(1024)S(1)} %broadcast_divide_fusion) | copy-start | bytes 12292
  73.7 12.1 %all-to-all-start.4 = ((bf16[8,24,1024]{2,1,0:T(8,128)(2,1)}), bf16[8,24,1024]{2,1,0:T(8,128)(2,1)S(1)}, u32[]{:S(2)}, u32[]{:S(2)}) async-start(bf16[8,24,1024]{2,1,0:T(8,128)(2,1)} %bitcast.151), calls=%async_computation.4 | async-start | bytes 786432 | tf_op jit(solution)/shard_map/near_scatter/all_to_all | solution.py:13
  78.3 0.6 copy-start.17
  85.8 27.4 %copy-start.3 = (bf16[8,3,1024]{2,1,0:T(4,128)(2,1)S(1)}, bf16[8,3,1024]{2,1,0:T(4,128)(2,1)}, u32[]{:S(2)}) copy-start(bf16[8,3,1024]{2,1,0:T(4,128)(2,1)} %copy-done.2) | copy-start | bytes 147460
  85.8 27.4 %copy-start.12 = (f32[1024]{0:T(1024)S(1)}, f32[1024]{0:T(1024)}, u32[]{:S(2)}) copy-start(f32[1024]{0:T(1024)} %copy-done.11) | copy-start | bytes 12292
  85.9 0.6 copy-start.4
  113.3 12.3 %copy-start.10 = (f32[1024]{0:T(1024)S(1)}, f32[1024]{0:T(1024)}, u32[]{:S(2)}) copy-start(f32[1024]{0:T(1024)} %copy-done.9) | copy-start | bytes 12292
  137.7 21.2 %copy-start.16 = (pred[24]{0:T(512)(128)(4,1)S(1)}, pred[24]{0:T(512)(128)(4,1)}, u32[]{:S(2)}) copy-start(pred[24]{0:T(512)(128)(4,1)} %broadcast_in_dim.161) | copy-start | bytes 76
  158.9 0.6 copy-start.5
  187.7 0.7 copy-start.1
  213.6 15.5 %copy-start.18 = (pred[8]{0:T(512)(128)(4,1)S(1)}, pred[8]{0:T(512)(128)(4,1)}, u32[]{:S(2)}) copy-start(pred[8]{0:T(512)(128)(4,1)} %copy-done.17) | copy-start | bytes 28
  213.9 41.5 %copy-start.7 = (f32[3,3,1024]{2,0,1:T(4,128)S(1)}, f32[3,3,1024]{2,0,1:T(4,128)}, u32[]{:S(2)}) copy-start(f32[3,3,1024]{2,0,1:T(4,128)} %copy-done.6) | copy-start | bytes 110596
  213.9 41.5 %copy-start.8 = (f32[3,1024]{1,0:T(4,128)S(1)}, f32[3,1024]{1,0:T(4,128)}, u32[]{:S(2)}) copy-start(f32[3,1024]{1,0:T(4,128)} %get-tuple-element.13) | copy-start | bytes 36868
  214.0 41.5 %copy-start.14 = (bf16[3,1024]{1,0:T(4,128)(2,1)S(1)}, bf16[3,1024]{1,0:T(4,128)(2,1)}, u32[]{:S(2)}) copy-start(bf16[3,1024]{1,0:T(4,128)(2,1)} %param.8) | copy-start | bytes 18436
  224.5 12.2 %all-to-all-start.14 = ((bf16[8,24,1024]{2,1,0:T(8,128)(2,1)}), bf16[8,24,1024]{2,1,0:T(8,128)(2,1)S(1)}, u32[]{:S(2)}, u32[]{:S(2)}) async-start(bf16[8,24,1024]{2,1,0:T(8,128)(2,1)} %bitcast.35), calls=%async_computation.14 | async-start | bytes 786432 | tf_op jit(solution)/shard_map/near_scatter/all_to_all | solution.py:13
  237.4 18.0 %all-to-all-start.15 = ((bf16[8,3,1024]{2,1,0:T(4,128)(2,1)}), bf16[8,3,1024]{2,1,0:T(4,128)(2,1)S(1)}, u32[]{:S(2)}, u32[]{:S(2)}) async-start(bf16[8,3,1024]{2,1,0:T(4,128)(2,1)} %copy.59), calls=%async_computation.15 | async-start | bytes 131072 | tf_op jit(solution)/shard_map/far_scatter/all_to_all | solution.py:13

commit v3 on v2

--- a/solution.py
+++ b/solution.py
@@ -1,6 +1,8 @@
 import jax
 import jax.numpy as jnp
 from jax import lax
+from jax.experimental import pallas as pl
+from jax.experimental.pallas import tpu as pltpu
 from jax.sharding import Mesh, PartitionSpec as P
 
 D = 8192
@@ -17,31 +19,77 @@
     return swap(jnp.broadcast_to(array[None], (8,) + array.shape), axes)
 
 
-def attention(queries, new_kv, kv_cache, lengths):
+def attention_kernel(lengths_ref, x_ref, queries_ref, new_ref, cache_ref, out_ref, first_ref, spread_ref):
+    steps, _, heads, size = queries_ref.shape
+    rows = steps * heads
+    scale = size ** (-0.5)
+    wide = queries_ref[...].astype(jnp.float32).reshape(rows, size)
+    keys = cache_ref[0, 0, 0]
+    values = cache_ref[0, 0, 1]
+    scores = lax.dot_general(
+        wide.astype(jnp.bfloat16), keys, (((1,), (1,)), ((), ())), preferred_element_type=jnp.float32
+    )
+    position = lax.broadcasted_iota(jnp.int32, scores.shape, 1)
+    scores = jnp.where(position < lengths_ref[pl.program_id(0)], scores * scale, -1e30)
+    top = jnp.max(scores, axis=1, keepdims=True)
+    row_step = lax.broadcasted_iota(jnp.int32, (rows, 1), 0) // heads
+    new = new_ref[...].astype(jnp.float32)
+    fresh = []
+    for step in range(steps):
+        score = jnp.sum(wide * new[step, 0, 0, 0:1], axis=1, keepdims=True) * scale
+        fresh.append(jnp.where(row_step >= step, score, -1e30))
+        top = jnp.maximum(top, fresh[-1])
+    weights = jnp.exp(scores - top)
+    total = jnp.sum(weights, axis=1, keepdims=True)
+    for step in range(steps):
+        fresh[step] = jnp.exp(fresh[step] - top)
+        total = total + fresh[step]
+    out = jnp.dot((weights / total).astype(jnp.bfloat16), values, preferred_element_type=jnp.float32)
+    for step in range(steps):
+        prob = (fresh[step] / total).astype(jnp.bfloat16).astype(jnp.float32)
+        out = out + prob * new[step, 0, 0, 1:2]
+    out_ref[...] = out.reshape(out_ref.shape)
+    state = x_ref[...].astype(jnp.float32)
+    row = lax.broadcasted_iota(jnp.int32, state.shape, 0)
+    state = jnp.sum(jnp.where(row == pl.program_id(0), state, 0.0), axis=0, keepdims=True)
+    state = jnp.concatenate([state[:, k * size : (k + 1) * size] for k in range(heads)], axis=0)
+    first = state + out[:heads]
+    first_ref[0] = first
+    spread_ref[...] = jnp.broadcast_to(first.astype(jnp.bfloat16), spread_ref.shape)
+
+
+def attention(x_init, queries, new_kv, kv_cache, lengths):
     steps, requests, heads, size = queries.shape
     cache_length = kv_cache.shape[3]
-    keys = kv_cache[:, 0, 0]
-    values = kv_cache[:, 0, 1]
-    rows = queries.transpose(1, 0, 2, 3).reshape(requests, steps * heads, size)
-    scale = size ** (-0.5)
-    scores = jnp.einsum("rqd,rld->rql", rows, keys, preferred_element_type=jnp.float32) * scale
-    live = jnp.arange(cache_length, dtype=jnp.int32)[None, :] < lengths[:, None]
-    scores = jnp.where(live[:, None, :], scores, -1e30)
-    fresh_keys = new_kv[:, :, 0, 0]
-    fresh_values = new_kv[:, :, 0, 1]
-    fresh = jnp.einsum("rqd,nrd->rqn", rows, fresh_keys, preferred_element_type=jnp.float32) * scale
-    row_step = jnp.arange(steps * heads, dtype=jnp.int32) // heads
-    seen = jnp.arange(steps, dtype=jnp.int32)[None, :] <= row_step[:, None]
-    fresh = jnp.where(seen[None], fresh, -1e30)
-    top = jnp.maximum(jnp.max(scores, axis=-1), jnp.max(fresh, axis=-1))[..., None]
-    cache_exp = jnp.exp(scores - top)
-    fresh_exp = jnp.where(seen[None], jnp.exp(fresh - top), 0.0)
-    total = jnp.sum(cache_exp, axis=-1, keepdims=True) + jnp.sum(fresh_exp, axis=-1, keepdims=True)
-    cache_probs = (cache_exp / total).astype(jnp.bfloat16)
-    fresh_probs = (fresh_exp / total).astype(jnp.bfloat16)
-    out = jnp.einsum("rql,rld->rqd", cache_probs, values, preferred_element_type=jnp.float32)
-    out = out + jnp.einsum("rqn,nrd->rqd", fresh_probs, fresh_values, preferred_element_type=jnp.float32)
-    return out.reshape(requests, steps, heads * size).transpose(1, 0, 2)
+    out, first, spread_first = pl.pallas_call(
+        attention_kernel,
+        grid_spec=pltpu.PrefetchScalarGridSpec(
+            num_scalar_prefetch=1,
+            grid=(requests,),
+            in_specs=[
+                pl.BlockSpec((requests, heads * size), lambda r, _: (0, 0)),
+                pl.BlockSpec((steps, 1, heads, size), lambda r, _: (0, r, 0, 0)),
+                pl.BlockSpec((steps, 1, 1, 2, size), lambda r, _: (0, r, 0, 0, 0)),
+                pl.BlockSpec((1, 1, 2, cache_length, size), lambda r, _: (r, 0, 0, 0, 0)),
+            ],
+            out_specs=[
+                pl.BlockSpec((steps, 1, heads, size), lambda r, _: (0, r, 0, 0)),
+                pl.BlockSpec((1, heads, size), lambda r, _: (r, 0, 0)),
+                pl.BlockSpec((8, 1, heads, size), lambda r, _: (0, r, 0, 0)),
+            ],
+        ),
+        out_shape=[
+            jax.ShapeDtypeStruct((steps, requests, heads, size), jnp.float32),
+            jax.ShapeDtypeStruct((requests, heads, size), jnp.float32),
+            jax.ShapeDtypeStruct((8, requests, heads, size), jnp.bfloat16),
+        ],
+        compiler_params=pltpu.CompilerParams(vmem_limit_bytes=56 * 2**20),
+    )(lengths, x_init, queries, new_kv, kv_cache)
+    return (
+        out.reshape(steps, requests, heads * size),
+        first.reshape(requests, heads * size),
+        spread_first.reshape(8, requests * heads, size),
+    )
 
 
 def place_rows(mine, far_index):
@@ -63,15 +111,14 @@
     units = w_gate_up.shape[2]
     w_flat = w_gate_up.reshape(width, 2 * units)
     with jax.named_scope("attention"):
-        attended = attention(queries, new_kv, kv_cache, lengths)
+        attended, own_first, first = attention(x_init, queries, new_kv, kv_cache, lengths)
     gain = norm_gain.astype(jnp.float32)
     inverse_gain = 1.0 / gain
     far_index = lax.axis_index(FAR)
-    own_first = x_init.astype(jnp.float32) + attended[0]
     with jax.named_scope("start_far_gather"):
-        blocks = spread(own_first.astype(jnp.bfloat16), FAR)
+        blocks = swap(first, FAR)
     blocks, w_flat = lax.optimization_barrier((blocks, w_flat))
-    blocks = blocks.astype(jnp.float32).transpose(1, 0, 2)
+    blocks = blocks.reshape(8, requests, width).astype(jnp.float32).transpose(1, 0, 2)
 
     def near_gather(hidden_in):
         with jax.named_scope("near_gather"):
@@ -122,7 +169,8 @@
         near_sum = jnp.sum(down.astype(jnp.float32), axis=0).astype(jnp.bfloat16)
         count = near_sum.shape[0] // 8
         with jax.named_scope("far_scatter"):
-            return swap(near_sum.reshape(count, 8, width).transpose(1, 0, 2), FAR)
+            parts = near_sum.reshape(count, 8, width).transpose(1, 0, 2)
+            return swap(parts.reshape(8, 8 * count, width // 8), FAR)
 
     chains = ((0, 3),)
     hidden_in = [blocks[a:b].reshape((b - a) * 8, width) for a, b in chains]
@@ -144,7 +192,10 @@
                 for near_sum, sent, got in data
             ]
         else:
-            own_down = [jnp.sum(far_scatter(d).astype(jnp.float32), axis=0) for d in data]
+            own_down = [
+                jnp.sum(far_scatter(d).astype(jnp.float32), axis=0).reshape(h.shape)
+                for d, h in zip(data, own_hidden)
+            ]
         state = [(h + d).astype(jnp.bfloat16) for h, d in zip(own_hidden, own_down)]
         results.append(jnp.concatenate(state, axis=0))
         if step + 1 < steps:

time: 258 us -> 255 us (0.988)
  local copies, waits for them, and re-layouts: 14 us -> 8.14 us
  Pallas kernels: 0 us -> 4.65 us
  matrix products: 8.65 us -> 4.39 us
    pallas_call x0 -> x1, Pallas kernels: none -> 4.65 us  [attention(): pl.pallas_call(attention_kernel, grid_spec=pltpu.PrefetchScalarGridSpec(n...]
    dot_general x4 -> x0, matrix products: 4.26 us -> none  [the longest x1 1.77 us: attention(): jnp.einsum('rqd,rld->rql', rows, keys, preferred_element_type=jnp.float32)]
    unnamed x39 -> x17, local copies, waits for them, and re-layouts: 5.19 us -> 3.39 us
  transfers between devices with their start and end apart: 5 -> 5, of which waited for: 5 -> 5; matrix products, arithmetic and copies ran while one was open for 3% -> 2% of each run, Pallas kernels for 0% -> 0%
where the time goes in v3:
time: 255 us; the launch traced here: 253 us
  blocking collectives  154 us (60%)
  waiting for transfers between devices  42.2 us (17%)
  starting transfers between devices  34.1 us (13%)
  local copies, waits for them, and re-layouts  8.14 us (3%)
  other arithmetic  5.14 us (2%)
  Pallas kernels  4.65 us (2%)
  matrix products  4.39 us (2%)
    all_to_all x11, blocking collectives, swap(): return lax.all_to_all(array, axes, 0, 0, tiled=True)  154 us
    all_to_all x5, waiting for transfers between devices, swap(): return lax.all_to_all(array, axes, 0, 0, tiled=True)  42.2 us
    all_to_all x5, starting transfers between devices, swap(): return lax.all_to_all(array, axes, 0, 0, tiled=True)  34.1 us
  transfers between devices with their start and end apart: 5, of which 5 were waited for; matrix products, arithmetic and copies ran while one was open for 2% of the time, Pallas kernels for 0%

profile of v3, /device:TPU:32, one launch (start us, length us, event | category | flops | bytes accessed | tf_op | source)
XLA Modules:
  0.0 253.4 jit_solution(958839054059011572)
XLA Ops:
  0.0 4.6 %attention.1 = (f32[3,3,8,128]{3,2,1,0:T(8,128)}, f32[3,8,128]{2,1,0:T(8,128)}, bf16[8,3,8,128]{3,2,1,0:T(8,128)(2,1)}) custom-call(s32[3]{0:T(128)} %lengths_ref.1, bf16[3,1024]{1,0:T(4,128)(2,1)} %x_ref.1, bf16[3,3,8,128]{3,2,1,0:T(8,128)(2,1)} %queries_ref.1, bf16[3,3,1,2,128]{4,3,2,1,0:T(2,128)(2,1)} %new_ref.1, bf16[3,1,2,1024,128]{4,3,2,1,0:T(8,128)(2,1)} %cache_ref.1), custom_call_target="tpu_custom_call" | custom-call | tf_op jit(solution)/shard_map/attention/pallas_call | solution.py:64
  4.7 14.2 %all-to-all-start = ((bf16[8,24,128]{2,1,0:T(8,128)(2,1)}), bf16[8,24,128]{2,1,0:T(8,128)(2,1)S(1)}, u32[]{:S(2)}, u32[]{:S(2)}) async-start(bf16[8,24,128]{2,1,0:T(8,128)(2,1)} %bitcast.117), calls=%async_computation | async-start | bytes 98304 | tf_op jit(solution)/shard_map/start_far_gather/all_to_all | solution.py:15
  18.8 0.7 convert_element_type.232
  19.5 2.2 copy.46
  21.7 10.2 %all-to-all-done = bf16[8,24,128]{2,1,0:T(8,128)(2,1)S(1)} async-done(((bf16[8,24,128]{2,1,0:T(8,128)(2,1)}), bf16[8,24,128]{2,1,0:T(8,128)(2,1)S(1)}, u32[]{:S(2)}, u32[]{:S(2)}) %all-to-all-start) | async-done | bytes 49184 | tf_op jit(solution)/shard_map/start_far_gather/all_to_all | solution.py:15
  32.0 0.0 copy-start.1
  32.0 0.1 fusion.7
  32.0 0.8 broadcast_in_dim.104
  32.8 0.0 copy-done.1
  32.8 5.8 %all-to-all-start.1 = ((bf16[8,24,1024]{2,1,0:T(8,128)(2,1)}), bf16[8,24,1024]{2,1,0:T(8,128)(2,1)S(1)}, u32[]{:S(2)}, u32[]{:S(2)}) async-start(bf16[8,24,1024]{2,1,0:T(8,128)(2,1)} %broadcast_in_dim.104), calls=%async_computation.1 | async-start | bytes 786432 | tf_op jit(solution)/shard_map/near_gather/all_to_all | solution.py:15
  38.6 6.8 %all-to-all-done.1 = bf16[8,24,1024]{2,1,0:T(8,128)(2,1)S(1)} async-done(((bf16[8,24,1024]{2,1,0:T(8,128)(2,1)}), bf16[8,24,1024]{2,1,0:T(8,128)(2,1)S(1)}, u32[]{:S(2)}, u32[]{:S(2)}) %all-to-all-start.1) | async-done | bytes 393248 | tf_op jit(solution)/shard_map/near_gather/all_to_all | solution.py:15
  45.4 0.1 multiply_multiply_fusion.2
  45.6 0.6 convolution_convert_fusion.5
  46.2 13.8 %all_to_all.80 = bf16[8,24,1152]{2,1,0:T(8,128)(2,1)S(1)} all-to-all(bf16[8,24,1152]{2,1,0:T(8,128)(2,1)S(1)} %pad_maximum_fusion), channel_id=1, replica_groups=mesh['x'=4,'za'=2,'zb'=2,'zh'=4,'y'=4,'c'=2] {'y','c'}, dimensions={0} | all-to-all | bytes 884736 | tf_op jit(solution)/shard_map/tp_scatter/all_to_all | solution.py:15
  60.0 0.1 convert_reduce_fusion.2
  60.0 0.1 slice_reduce_fusion.2
  60.1 0.1 slice_multiply_fusion.2
  60.3 9.2 %all_to_all.81 = bf16[8,24,512]{2,1,0:T(8,128)(2,1)S(1)} all-to-all(bf16[8,24,512]{2,1,0:T(8,128)(2,1)S(1)} %broadcast_in_dim.105), channel_id=1, replica_groups=mesh['x'=4,'za'=2,'zb'=2,'zh'=4,'y'=4,'c'=2] {'y','c'}, dimensions={0} | all-to-all | bytes 393216 | tf_op jit(solution)/shard_map/tp_gather/all_to_all | solution.py:15
  69.5 1.1 convolution_convert_fusion.4
  70.7 5.2 %all-to-all-start.4 = ((bf16[8,24,1024]{2,1,0:T(8,128)(2,1)}), bf16[8,24,1024]{2,1,0:T(8,128)(2,1)}, u32[]{:S(2)}, u32[]{:S(2)}) async-start(bf16[8,24,1024]{2,1,0:T(8,128)(2,1)} %bitcast.102), calls=%async_computation.4 | async-start | bytes 786432 | tf_op jit(solution)/shard_map/near_scatter/all_to_all | solution.py:15
  75.8 0.1 broadcast_in_dim.107
  75.9 7.5 %all-to-all-done.4 = bf16[8,24,1024]{2,1,0:T(8,128)(2,1)} async-done(((bf16[8,24,1024]{2,1,0:T(8,128)(2,1)}), bf16[8,24,1024]{2,1,0:T(8,128)(2,1)}, u32[]{:S(2)}, u32[]{:S(2)}) %all-to-all-start.4) | async-done | bytes 393248 | tf_op jit(solution)/shard_map/near_scatter/all_to_all | solution.py:15
  83.5 1.1 convert_reduce_fusion.6
  84.5 0.1 fusion.6
  84.6 25.8 %all_to_all.82 = bf16[8,24,1024]{2,1,0:T(8,128)(2,1)S(1)} all-to-all(bf16[8,24,1024]{2,1,0:T(8,128)(2,1)S(1)} %broadcast_in_dim.113), channel_id=1, replica_groups=mesh['x'=4,'za'=2,'zb'=2,'zh'=4,'y'=4,'c'=2] {'za','zh'}, dimensions={0} | all-to-all | bytes 786432 | tf_op jit(solution)/shard_map/far_exchange/all_to_all | solution.py:15
  110.5 0.1 convert_reduce_fusion.5
  110.5 0.1 multiply_convert_fusion.1
  110.6 0.6 copy-done.3
  111.3 11.7 %all_to_all.83 = bf16[8,24,1024]{2,1,0:T(8,128)(2,1)S(1)} all-to-all(bf16[8,24,1024]{2,1,0:T(8,128)(2,1)S(1)} %broadcast_in_dim.116), channel_id=1, replica_groups=mesh['x'=4,'za'=2,'zb'=2,'zh'=4,'y'=4,'c'=2] {'x','zb'}, dimensions={0} | all-to-all | bytes 786432 | tf_op jit(solution)/shard_map/near_gather/all_to_all | solution.py:15
  122.9 0.6 convolution_convert_fusion.3
  123.5 0.1 multiply_multiply_fusion.1
  123.7 11.9 %all_to_all.84 = bf16[8,24,1152]{2,1,0:T(8,128)(2,1)S(1)} all-to-all(bf16[8,24,1152]{2,1,0:T(8,128)(2,1)S(1)} %pad_maximum_fusion.1), channel_id=1, replica_groups=mesh['x'=4,'za'=2,'zb'=2,'zh'=4,'y'=4,'c'=2] {'y','c'}, dimensions={0} | all-to-all | bytes 884736 | tf_op jit(solution)/shard_map/tp_scatter/all_to_all | solution.py:15
  135.6 0.1 convert_reduce_fusion.1
  135.7 0.1 slice_reduce_fusion.1
  135.8 0.1 slice_multiply_fusion.1
  135.9 9.2 %all_to_all.85 = bf16[8,24,512]{2,1,0:T(8,128)(2,1)S(1)} all-to-all(bf16[8,24,512]{2,1,0:T(8,128)(2,1)S(1)} %broadcast_in_dim.117), channel_id=1, replica_groups=mesh['x'=4,'za'=2,'zb'=2,'zh'=4,'y'=4,'c'=2] {'y','c'}, dimensions={0} | all-to-all | bytes 393216 | tf_op jit(solution)/shard_map/tp_gather/all_to_all | solution.py:15
  145.1 0.4 convolution_convert_fusion.2
  145.5 11.2 %all_to_all.86 = bf16[8,24,1024]{2,1,0:T(8,128)(2,1)S(1)} all-to-all(bf16[8,24,1024]{2,1,0:T(8,128)(2,1)S(1)} %bitcast.103), channel_id=1, replica_groups=mesh['x'=4,'za'=2,'zb'=2,'zh'=4,'y'=4,'c'=2] {'x','zb'}, dimensions={0} | all-to-all | bytes 786432 | tf_op jit(solution)/shard_map/near_scatter/all_to_all | solution.py:15
  156.7 0.1 convert_reduce_fusion.4
  156.8 0.1 fusion.4
  156.9 28.1 %all_to_all.87 = bf16[8,24,1024]{2,1,0:T(8,128)(2,1)S(1)} all-to-all(bf16[8,24,1024]{2,1,0:T(8,128)(2,1)S(1)} %broadcast_in_dim.121), channel_id=1, replica_groups=mesh['x'=4,'za'=2,'zb'=2,'zh'=4,'y'=4,'c'=2] {'za','zh'}, dimensions={0} | all-to-all | bytes 786432 | tf_op jit(solution)/shard_map/far_exchange/all_to_all | solution.py:15
  185.0 0.1 convert_reduce_fusion.3
  185.0 0.1 multiply_convert_fusion
  185.1 0.6 copy-done.4
  185.7 12.1 %all_to_all.88 = bf16[8,24,1024]{2,1,0:T(8,128)(2,1)S(1)} all-to-all(bf16[8,24,1024]{2,1,0:T(8,128)(2,1)S(1)} %broadcast_in_dim.122), channel_id=1, replica_groups=mesh['x'=4,'za'=2,'zb'=2,'zh'=4,'y'=4,'c'=2] {'x','zb'}, dimensions={0} | all-to-all | bytes 786432 | tf_op jit(solution)/shard_map/near_gather/all_to_all | solution.py:15
  197.9 0.6 convolution_convert_fusion.1
  198.4 0.1 multiply_multiply_fusion
  198.7 12.2 %all_to_all.89 = bf16[8,24,1152]{2,1,0:T(8,128)(2,1)S(1)} all-to-all(bf16[8,24,1152]{2,1,0:T(8,128)(2,1)S(1)} %pad_maximum_fusion.2), channel_id=1, replica_groups=mesh['x'=4,'za'=2,'zb'=2,'zh'=4,'y'=4,'c'=2] {'y','c'}, dimensions={0} | all-to-all | bytes 884736 | tf_op jit(solution)/shard_map/tp_scatter/all_to_all | solution.py:15
  210.9 0.1 convert_reduce_fusion
  211.0 0.1 slice_reduce_fusion
  211.1 0.1 slice_multiply_fusion
  211.2 9.2 %all_to_all.90 = bf16[8,24,512]{2,1,0:T(8,128)(2,1)S(1)} all-to-all(bf16[8,24,512]{2,1,0:T(8,128)(2,1)S(1)} %broadcast_in_dim.123), channel_id=1, replica_groups=mesh['x'=4,'za'=2,'zb'=2,'zh'=4,'y'=4,'c'=2] {'y','c'}, dimensions={0} | all-to-all | bytes 393216 | tf_op jit(solution)/shard_map/tp_gather/all_to_all | solution.py:15
  220.4 1.1 convolution_convert_fusion
  221.6 4.6 %all-to-all-start.14 = ((bf16[8,24,1024]{2,1,0:T(8,128)(2,1)}), bf16[8,24,1024]{2,1,0:T(8,128)(2,1)S(1)}, u32[]{:S(2)}, u32[]{:S(2)}) async-start(bf16[8,24,1024]{2,1,0:T(8,128)(2,1)} %bitcast.28), calls=%async_computation.14 | async-start | bytes 786432 | tf_op jit(solution)/shard_map/near_scatter/all_to_all | solution.py:15
  226.2 0.6 dynamic-slice
  226.9 1.1 constant_dynamic-slice_fusion.3
  228.1 5.6 %all-to-all-done.14 = bf16[8,24,1024]{2,1,0:T(8,128)(2,1)S(1)} async-done(((bf16[8,24,1024]{2,1,0:T(8,128)(2,1)}), bf16[8,24,1024]{2,1,0:T(8,128)(2,1)S(1)}, u32[]{:S(2)}, u32[]{:S(2)}) %all-to-all-start.14) | async-done | bytes 393248 | tf_op jit(solution)/shard_map/near_scatter/all_to_all | solution.py:15
  233.8 0.1 reduce_sum.153
  233.9 0.7 reshape.441
  234.5 4.4 %all-to-all-start.15 = ((bf16[8,24,128]{2,1,0:T(8,128)(2,1)}), bf16[8,24,128]{2,1,0:T(8,128)(2,1)S(1)}, u32[]{:S(2)}, u32[]{:S(2)}) async-start(bf16[8,24,128]{2,1,0:T(8,128)(2,1)} %reshape.441), calls=%async_computation.15 | async-start | bytes 98304 | tf_op jit(solution)/shard_map/far_scatter/all_to_all | solution.py:15
  238.9 1.1 constant_dynamic-slice_fusion
  240.1 12.0 %all-to-all-done.15 = bf16[8,24,128]{2,1,0:T(8,128)(2,1)S(1)} async-done(((bf16[8,24,128]{2,1,0:T(8,128)(2,1)}), bf16[8,24,128]{2,1,0:T(8,128)(2,1)S(1)}, u32[]{:S(2)}, u32[]{:S(2)}) %all-to-all-start.15) | async-done | bytes 49184 | tf_op jit(solution)/shard_map/far_scatter/all_to_all | solution.py:15
  252.1 0.7 fusion.20
  252.7 0.6 pad_maximum_fusion.3
  (47 shorter events, 0.9 us)
Async XLA Ops:
  0.0 69.5 %copy-start = (bf16[512,1024]{1,0:T(8,128)(2,1)S(1)}, bf16[512,1024]{1,0:T(8,128)(2,1)}, u32[]{:S(2)}) copy-start(bf16[512,1024]{1,0:T(8,128)(2,1)} %param.15) | copy-start | bytes 3145732
  4.7 27.3 %all-to-all-start = ((bf16[8,24,128]{2,1,0:T(8,128)(2,1)}), bf16[8,24,128]{2,1,0:T(8,128)(2,1)S(1)}, u32[]{:S(2)}, u32[]{:S(2)}) async-start(bf16[8,24,128]{2,1,0:T(8,128)(2,1)} %bitcast.117), calls=%async_computation | async-start | bytes 98304 | tf_op jit(solution)/shard_map/start_far_gather/all_to_all | solution.py:15
  19.5 19.1 %copy-start.7 = (bf16[1024]{0:T(1024)(128)(2,1)S(1)}, bf16[1024]{0:T(1024)(128)(2,1)}, u32[]{:S(2)}) copy-start(bf16[1024]{0:T(1024)(128)(2,1)} %param.13) | copy-start | bytes 6148
  32.0 0.9 copy-start.1
  32.8 12.6 %all-to-all-start.1 = ((bf16[8,24,1024]{2,1,0:T(8,128)(2,1)}), bf16[8,24,1024]{2,1,0:T(8,128)(2,1)S(1)}, u32[]{:S(2)}, u32[]{:S(2)}) async-start(bf16[8,24,1024]{2,1,0:T(8,128)(2,1)} %broadcast_in_dim.104), calls=%async_computation.1 | async-start | bytes 786432 | tf_op jit(solution)/shard_map/near_gather/all_to_all | solution.py:15
  60.0 16.0 %copy-start.5 = (f32[3,3,8,128]{3,2,1,0:T(8,128)S(1)}, f32[3,3,8,128]{3,2,1,0:T(8,128)}, u32[]{:S(2)}) copy-start(f32[3,3,8,128]{3,2,1,0:T(8,128)} %get-tuple-element.14) | copy-start | bytes 110596
  69.5 41.0 %copy-start.2 = (f32[8,3,1024]{2,1,0:T(4,128)S(1)}, f32[8,3,1024]{2,1,0:T(4,128)}, u32[]{:S(2)}) copy-start(f32[8,3,1024]{2,1,0:T(4,128)} %copy-done.1) | copy-start | bytes 294916
  70.7 12.8 %all-to-all-start.4 = ((bf16[8,24,1024]{2,1,0:T(8,128)(2,1)}), bf16[8,24,1024]{2,1,0:T(8,128)(2,1)}, u32[]{:S(2)}, u32[]{:S(2)}) async-start(bf16[8,24,1024]{2,1,0:T(8,128)(2,1)} %bitcast.102), calls=%async_computation.4 | async-start | bytes 786432 | tf_op jit(solution)/shard_map/near_scatter/all_to_all | solution.py:15
  110.5 0.7 copy-start.3
  185.0 0.7 copy-start.4
  210.9 16.0 %copy-start.6 = (f32[3,8,128]{2,1,0:T(8,128)S(1)}, f32[3,8,128]{2,1,0:T(8,128)}, u32[]{:S(2)}) copy-start(f32[3,8,128]{2,1,0:T(8,128)} %get-tuple-element.10) | copy-start | bytes 36868
  221.6 12.2 %all-to-all-start.14 = ((bf16[8,24,1024]{2,1,0:T(8,128)(2,1)}), bf16[8,24,1024]{2,1,0:T(8,128)(2,1)S(1)}, u32[]{:S(2)}, u32[]{:S(2)}) async-start(bf16[8,24,1024]{2,1,0:T(8,128)(2,1)} %bitcast.28), calls=%async_computation.14 | async-start | bytes 786432 | tf_op jit(solution)/shard_map/near_scatter/all_to_all | solution.py:15
  234.5 17.5 %all-to-all-start.15 = ((bf16[8,24,128]{2,1,0:T(8,128)(2,1)}), bf16[8,24,128]{2,1,0:T(8,128)(2,1)S(1)}, u32[]{:S(2)}, u32[]{:S(2)}) async-start(bf16[8,24,128]{2,1,0:T(8,128)(2,1)} %reshape.441), calls=%async_computation.15 | async-start | bytes 98304 | tf_op jit(solution)/shard_map/far_scatter/all_to_all | solution.py:15

commit v4 on v3

--- a/solution.py
+++ b/solution.py
@@ -6,13 +6,33 @@
 from jax.sharding import Mesh, PartitionSpec as P
 
 D = 8192
-NEAR = ("x", "zb")
-FAR = ("za", "zh")
-TP = ("y", "c")
-
-
-def swap(array, axes):
-    return lax.all_to_all(array, axes, 0, 0, tiled=True)
+TP = "t"
+
+
+def owner(x, za, zb, zh):
+    return ((x * 2 + za) * 2 + zb) * 4 + zh
+
+
+def half(side, zh):
+    return side ^ (zh >> 1)
+
+
+NEAR = [
+    [owner(x, za, half(side, zh), zh) for x in range(4) for side in range(2)]
+    for za in range(2)
+    for zh in range(4)
+]
+FAR = [
+    [owner(x, za, half(side, zh), zh) for za in range(2) for zh in range(4)]
+    for x in range(4)
+    for side in range(2)
+]
+
+
+def swap(array, group):
+    if group is TP:
+        return lax.all_to_all(array, TP, 0, 0, tiled=True)
+    return lax.all_to_all(array, "r", 0, 0, axis_index_groups=group, tiled=True)
 
 
 def spread(array, axes):
@@ -114,11 +134,15 @@
         attended, own_first, first = attention(x_init, queries, new_kv, kv_cache, lengths)
     gain = norm_gain.astype(jnp.float32)
     inverse_gain = 1.0 / gain
-    far_index = lax.axis_index(FAR)
+    place = lax.axis_index("r")
+    far_index = place // 8 % 2 * 4 + place % 4
     with jax.named_scope("start_far_gather"):
         blocks = swap(first, FAR)
-    blocks, w_flat = lax.optimization_barrier((blocks, w_flat))
+    placed = [place_rows(attended[step], far_index) for step in range(1, steps)]
+    ready = lax.optimization_barrier((blocks, w_flat, gain, inverse_gain, placed))
+    blocks, w_flat, gain, inverse_gain, placed = ready
     blocks = blocks.reshape(8, requests, width).astype(jnp.float32).transpose(1, 0, 2)
+    hidden_in = blocks.reshape(requests * 8, width)
 
     def near_gather(hidden_in):
         with jax.named_scope("near_gather"):
@@ -161,9 +185,11 @@
 
     def far_exchange(down, coming):
         near_sum = jnp.sum(down.astype(jnp.float32), axis=0)
-        sent = (near_sum + place_rows(coming, far_index)).astype(jnp.bfloat16)
+        exact = near_sum + coming
+        sent = lax.reduce_precision(exact, 8, 7)
+        residual = (exact - sent).astype(jnp.bfloat16)
         with jax.named_scope("far_exchange"):
-            return near_sum, sent, spread(sent, FAR)
+            return residual, spread(sent.astype(jnp.bfloat16), FAR)
 
     def far_scatter(down):
         near_sum = jnp.sum(down.astype(jnp.float32), axis=0).astype(jnp.bfloat16)
@@ -172,40 +198,35 @@
             parts = near_sum.reshape(count, 8, width).transpose(1, 0, 2)
             return swap(parts.reshape(8, 8 * count, width // 8), FAR)
 
-    chains = ((0, 3),)
-    hidden_in = [blocks[a:b].reshape((b - a) * 8, width) for a, b in chains]
-    own_hidden = [own_first[a:b] for a, b in chains]
+    exchanged = []
+    for step in range(steps):
+        hidden = swiglu(gate_up(near_gather(hidden_in)))
+        down = down_product(hidden)
+        if step + 1 < steps:
+            exchanged.append(far_exchange(down, placed[step]))
+            hidden_in = hidden_in + jnp.sum(exchanged[-1][1].astype(jnp.float32), axis=0)
+    down, exchanged = lax.optimization_barrier((down, exchanged))
+    last = far_scatter(down)
     results = []
     for step in range(steps):
-        data = [near_gather(h) for h in hidden_in]
-        data = [gate_up(d) for d in data]
-        data = [swiglu(d) for d in data]
-        data = [down_product(d) for d in data]
         if step + 1 < steps:
-            coming = [attended[step + 1, a:b] for a, b in chains]
-            data = [far_exchange(d, c) for d, c in zip(data, coming)]
-            hidden_in = [h + jnp.sum(d[2].astype(jnp.float32), axis=0) for h, d in zip(hidden_in, data)]
-            own_down = [
+            residual, got = exchanged[step]
+            own_down = (
                 jnp.sum(own_rows(got, far_index).astype(jnp.float32), axis=0)
-                - own_rows(sent, far_index).astype(jnp.float32)
-                + own_rows(near_sum, far_index)
-                for near_sum, sent, got in data
-            ]
+                + own_rows(residual, far_index).astype(jnp.float32)
+                - attended[step + 1]
+            )
         else:
-            own_down = [
-                jnp.sum(far_scatter(d).astype(jnp.float32), axis=0).reshape(h.shape)
-                for d, h in zip(data, own_hidden)
-            ]
-        state = [(h + d).astype(jnp.bfloat16) for h, d in zip(own_hidden, own_down)]
-        results.append(jnp.concatenate(state, axis=0))
-        if step + 1 < steps:
-            own_hidden = [s.astype(jnp.float32) + c for s, c in zip(state, coming)]
+            own_down = jnp.sum(last.astype(jnp.float32), axis=0).reshape(own_first.shape)
+        own_hidden = own_first if step == 0 else state.astype(jnp.float32) + attended[step]
+        state = (own_hidden + own_down).astype(jnp.bfloat16)
+        results.append(state)
     return jnp.stack(results)
 
 
 def solution(mesh):
-    fine = Mesh(mesh.devices.reshape(4, 2, 2, 4, 4, 2), ("x", "za", "zb", "zh", "y", "c"))
-    owners = ("x", "za", "zb", "zh")
+    fine = Mesh(mesh.devices.reshape(64, 8), ("r", "t"))
+    owners = "r"
     return jax.shard_map(
         on_device,
         mesh=fine,

time: 255 us -> 246 us (0.965)
  blocking collectives: 154 us -> 178 us
  waiting for transfers between devices: 42.2 us -> 25.2 us
  starting transfers between devices: 34.1 us -> 22 us
    all_to_all x11 -> x13, blocking collectives: 154 us -> 178 us  [the longest x7 113 us: swap(): return lax.all_to_all(array, 'r', 0, 0, axis_index_groups=group, tiled=True)]
    all_to_all x5 -> x3, waiting for transfers between devices: 42.2 us -> 25.2 us  [swap(): return lax.all_to_all(array, 'r', 0, 0, axis_index_groups=group, tiled=True)]
    all_to_all x5 -> x3, starting transfers between devices: 34.1 us -> 22 us  [swap(): return lax.all_to_all(array, 'r', 0, 0, axis_index_groups=group, tiled=True)]
  transfers between devices with their start and end apart: 5 -> 3, of which waited for: 5 -> 3; matrix products, arithmetic and copies ran while one was open for 2% -> 2% of each run, Pallas kernels for 0% -> 0%
where the time goes in v4:
time: 246 us; the launch traced here: 245 us
  blocking collectives  178 us (72%)
  waiting for transfers between devices  25.2 us (10%)
  starting transfers between devices  22 us (9%)
  local copies, waits for them, and re-layouts  6.72 us (3%)
  Pallas kernels  4.65 us (2%)
  other arithmetic  4.65 us (2%)
  matrix products  3.65 us (1%)
    all_to_all x7, blocking collectives, swap(): return lax.all_to_all(array, 'r', 0, 0, axis_index_groups=group, tiled=True)  113 us
    all_to_all x6, blocking collectives, swap(): return lax.all_to_all(array, TP, 0, 0, tiled=True)  65.2 us
    all_to_all x3, waiting for transfers between devices, swap(): return lax.all_to_all(array, 'r', 0, 0, axis_index_groups=group, tiled=True)  25.2 us
    all_to_all x3, starting transfers between devices, swap(): return lax.all_to_all(array, 'r', 0, 0, axis_index_groups=group, tiled=True)  22 us
  transfers between devices with their start and end apart: 3, of which 3 were waited for; matrix products, arithmetic and copies ran while one was open for 2% of the time, Pallas kernels for 0%

profile of v4, /device:TPU:32, one launch (start us, length us, event | category | flops | bytes accessed | tf_op | source)
XLA Modules:
  0.0 245.0 jit_solution(16171443868514065748)
XLA Ops:
  0.0 4.6 %attention.1 = (f32[3,3,8,128]{3,2,1,0:T(8,128)}, f32[3,8,128]{2,1,0:T(8,128)}, bf16[8,3,8,128]{3,2,1,0:T(8,128)(2,1)}) custom-call(s32[3]{0:T(128)} %lengths_ref.1, bf16[3,1024]{1,0:T(4,128)(2,1)} %x_ref.1, bf16[3,3,8,128]{3,2,1,0:T(8,128)(2,1)} %queries_ref.1, bf16[3,3,1,2,128]{4,3,2,1,0:T(2,128)(2,1)} %new_ref.1, bf16[3,1,2,1024,128]{4,3,2,1,0:T(8,128)(2,1)} %cache_ref.1), custom_call_target="tpu_custom_call" | custom-call | tf_op jit(solution)/shard_map/attention/pallas_call | solution.py:84
  4.7 13.7 %all-to-all-start = ((bf16[8,24,128]{2,1,0:T(8,128)(2,1)}), bf16[8,24,128]{2,1,0:T(8,128)(2,1)S(1)}, u32[]{:S(2)}, u32[]{:S(2)}) async-start(bf16[8,24,128]{2,1,0:T(8,128)(2,1)} %bitcast.103), calls=%async_computation | async-start | bytes 98304 | tf_op jit(solution)/shard_map/start_far_gather/all_to_all | solution.py:35
  18.4 2.2 copy.36
  20.6 0.0 copy-done.8
  20.6 0.6 fusion.17
  21.2 0.1 broadcast_in_dim.101
  21.3 0.7 bitcast_select_fusion
  22.1 8.1 %all-to-all-done = bf16[8,24,128]{2,1,0:T(8,128)(2,1)S(1)} async-done(((bf16[8,24,128]{2,1,0:T(8,128)(2,1)}), bf16[8,24,128]{2,1,0:T(8,128)(2,1)S(1)}, u32[]{:S(2)}, u32[]{:S(2)}) %all-to-all-start) | async-done | bytes 49184 | tf_op jit(solution)/shard_map/start_far_gather/all_to_all | solution.py:35
  30.2 0.0 copy-start.3
  30.2 0.1 fusion.5
  30.4 12.4 %all_to_all.80 = bf16[8,24,1024]{2,1,0:T(8,128)(2,1)S(1)} all-to-all(bf16[8,24,1024]{2,1,0:T(8,128)(2,1)S(1)} %broadcast_in_dim.110), channel_id=1, replica_groups={{0,32,128,160,256,288,384,416},{8,40,136,168,264,296,392,424},{48,16,17..., dimensions={0} | all-to-all | bytes 786432 | tf_op jit(solution)/shard_map/near_gather/all_to_all | solution.py:35
  42.7 0.1 multiply_multiply_fusion.2
  42.9 0.6 convolution_convert_fusion.5
  43.5 0.0 copy-done.3
  43.5 13.8 %all_to_all.81 = bf16[8,24,1152]{2,1,0:T(8,128)(2,1)S(1)} all-to-all(bf16[8,24,1152]{2,1,0:T(8,128)(2,1)S(1)} %pad_maximum_fusion), channel_id=1, replica_groups=mesh['attn'=16,'ffn'=4,'tp'=8] {'tp'}, dimensions={0} | all-to-all | bytes 884736 | tf_op jit(solution)/shard_map/tp_scatter/all_to_all | solution.py:34
  57.3 0.1 convert_reduce_fusion.2
  57.4 0.1 slice_reduce_fusion.2
  57.5 0.1 slice_multiply_fusion.2
  57.6 9.2 %all_to_all.82 = bf16[8,24,512]{2,1,0:T(8,128)(2,1)S(1)} all-to-all(bf16[8,24,512]{2,1,0:T(8,128)(2,1)S(1)} %broadcast_in_dim.111), channel_id=1, replica_groups=mesh['attn'=16,'ffn'=4,'tp'=8] {'tp'}, dimensions={0} | all-to-all | bytes 393216 | tf_op jit(solution)/shard_map/tp_gather/all_to_all | solution.py:34
  66.8 0.0 copy-done
  66.9 0.4 convolution_convert_fusion.4
  67.2 11.2 %all_to_all.83 = bf16[8,24,1024]{2,1,0:T(8,128)(2,1)S(1)} all-to-all(bf16[8,24,1024]{2,1,0:T(8,128)(2,1)S(1)} %bitcast.88), channel_id=1, replica_groups={{0,32,128,160,256,288,384,416},{8,40,136,168,264,296,392,424},{48,16,17..., dimensions={0} | all-to-all | bytes 786432 | tf_op jit(solution)/shard_map/near_scatter/all_to_all | solution.py:35
  78.4 0.1 convert_reduce_fusion.6
  78.5 0.6 fusion
  79.2 26.3 %all_to_all.84 = bf16[8,24,1024]{2,1,0:T(8,128)(2,1)S(1)} all-to-all(bf16[8,24,1024]{2,1,0:T(8,128)(2,1)S(1)} %broadcast_in_dim.112), channel_id=1, replica_groups={{0,8,48,56,64,72,112,120},{32,40,16,24,96,104,80,88},{128,136,176,184,1..., dimensions={0} | all-to-all | bytes 786432 | tf_op jit(solution)/shard_map/far_exchange/all_to_all | solution.py:35
  105.5 0.1 convert_reduce_fusion.5
  105.5 0.0 copy-done.4
  105.6 0.1 multiply_convert_fusion.1
  105.7 12.7 %all_to_all.85 = bf16[8,24,1024]{2,1,0:T(8,128)(2,1)S(1)} all-to-all(bf16[8,24,1024]{2,1,0:T(8,128)(2,1)S(1)} %broadcast_in_dim.113), channel_id=1, replica_groups={{0,32,128,160,256,288,384,416},{8,40,136,168,264,296,392,424},{48,16,17..., dimensions={0} | all-to-all | bytes 786432 | tf_op jit(solution)/shard_map/near_gather/all_to_all | solution.py:35
  118.4 0.1 multiply_multiply_fusion.1
  118.5 0.6 convolution_convert_fusion.3
  119.1 11.9 %all_to_all.86 = bf16[8,24,1152]{2,1,0:T(8,128)(2,1)S(1)} all-to-all(bf16[8,24,1152]{2,1,0:T(8,128)(2,1)S(1)} %pad_maximum_fusion.1), channel_id=1, replica_groups=mesh['attn'=16,'ffn'=4,'tp'=8] {'tp'}, dimensions={0} | all-to-all | bytes 884736 | tf_op jit(solution)/shard_map/tp_scatter/all_to_all | solution.py:34
  131.0 0.1 convert_reduce_fusion.1
  131.1 0.1 slice_reduce_fusion.1
  131.2 0.1 slice_multiply_fusion.1
  131.4 9.2 %all_to_all.87 = bf16[8,24,512]{2,1,0:T(8,128)(2,1)S(1)} all-to-all(bf16[8,24,512]{2,1,0:T(8,128)(2,1)S(1)} %broadcast_in_dim.114), channel_id=1, replica_groups=mesh['attn'=16,'ffn'=4,'tp'=8] {'tp'}, dimensions={0} | all-to-all | bytes 393216 | tf_op jit(solution)/shard_map/tp_gather/all_to_all | solution.py:34
  140.6 0.4 convolution_convert_fusion.2
  141.0 11.2 %all_to_all.88 = bf16[8,24,1024]{2,1,0:T(8,128)(2,1)S(1)} all-to-all(bf16[8,24,1024]{2,1,0:T(8,128)(2,1)S(1)} %bitcast.89), channel_id=1, replica_groups={{0,32,128,160,256,288,384,416},{8,40,136,168,264,296,392,424},{48,16,17..., dimensions={0} | all-to-all | bytes 786432 | tf_op jit(solution)/shard_map/near_scatter/all_to_all | solution.py:35
  152.2 0.1 convert_reduce_fusion.4
  152.2 0.6 fusion.1
  152.9 26.7 %all_to_all.89 = bf16[8,24,1024]{2,1,0:T(8,128)(2,1)S(1)} all-to-all(bf16[8,24,1024]{2,1,0:T(8,128)(2,1)S(1)} %broadcast_in_dim.115), channel_id=1, replica_groups={{0,8,48,56,64,72,112,120},{32,40,16,24,96,104,80,88},{128,136,176,184,1..., dimensions={0} | all-to-all | bytes 786432 | tf_op jit(solution)/shard_map/far_exchange/all_to_all | solution.py:35
  179.6 0.7 copy-done.1
  180.4 0.1 convert_reduce_fusion.3
  180.4 0.1 multiply_convert_fusion
  180.5 12.0 %all_to_all.90 = bf16[8,24,1024]{2,1,0:T(8,128)(2,1)S(1)} all-to-all(bf16[8,24,1024]{2,1,0:T(8,128)(2,1)S(1)} %broadcast_in_dim.116), channel_id=1, replica_groups={{0,32,128,160,256,288,384,416},{8,40,136,168,264,296,392,424},{48,16,17..., dimensions={0} | all-to-all | bytes 786432 | tf_op jit(solution)/shard_map/near_gather/all_to_all | solution.py:35
  192.6 0.1 multiply_multiply_fusion
  192.7 0.6 convolution_convert_fusion.1
  193.4 11.9 %all_to_all.91 = bf16[8,24,1152]{2,1,0:T(8,128)(2,1)S(1)} all-to-all(bf16[8,24,1152]{2,1,0:T(8,128)(2,1)S(1)} %pad_maximum_fusion.2), channel_id=1, replica_groups=mesh['attn'=16,'ffn'=4,'tp'=8] {'tp'}, dimensions={0} | all-to-all | bytes 884736 | tf_op jit(solution)/shard_map/tp_scatter/all_to_all | solution.py:34
  205.3 0.1 convert_reduce_fusion
  205.3 0.1 slice_reduce_fusion
  205.4 0.1 slice_multiply_fusion
  205.6 9.2 %all_to_all.92 = bf16[8,24,512]{2,1,0:T(8,128)(2,1)S(1)} all-to-all(bf16[8,24,512]{2,1,0:T(8,128)(2,1)S(1)} %broadcast_in_dim.117), channel_id=1, replica_groups=mesh['attn'=16,'ffn'=4,'tp'=8] {'tp'}, dimensions={0} | all-to-all | bytes 393216 | tf_op jit(solution)/shard_map/tp_gather/all_to_all | solution.py:34
  214.8 1.1 convolution_convert_fusion
  216.0 4.8 %all-to-all-start.14 = ((bf16[8,24,1024]{2,1,0:T(8,128)(2,1)}), bf16[8,24,1024]{2,1,0:T(8,128)(2,1)S(1)}, u32[]{:S(2)}, u32[]{:S(2)}) async-start(bf16[8,24,1024]{2,1,0:T(8,128)(2,1)} %bitcast.16), calls=%async_computation.14 | async-start | bytes 786432 | tf_op jit(solution)/shard_map/near_scatter/all_to_all | solution.py:35
  220.7 7.5 %all-to-all-done.14 = bf16[8,24,1024]{2,1,0:T(8,128)(2,1)S(1)} async-done(((bf16[8,24,1024]{2,1,0:T(8,128)(2,1)}), bf16[8,24,1024]{2,1,0:T(8,128)(2,1)S(1)}, u32[]{:S(2)}, u32[]{:S(2)}) %all-to-all-start.14) | async-done | bytes 393248 | tf_op jit(solution)/shard_map/near_scatter/all_to_all | solution.py:35
  228.3 0.1 reduce_sum.147
  228.4 0.7 reshape.380
  229.0 3.5 %all-to-all-start.15 = ((bf16[8,24,128]{2,1,0:T(8,128)(2,1)}), bf16[8,24,128]{2,1,0:T(8,128)(2,1)S(1)}, u32[]{:S(2)}, u32[]{:S(2)}) async-start(bf16[8,24,128]{2,1,0:T(8,128)(2,1)} %reshape.380), calls=%async_computation.15 | async-start | bytes 98304 | tf_op jit(solution)/shard_map/far_scatter/all_to_all | solution.py:35
  232.5 0.2 copy.29
  232.7 0.2 copy.25
  233.1 0.8 constant_dynamic-slice_fusion
  233.9 0.8 constant_dynamic-slice_fusion.1
  234.7 9.6 %all-to-all-done.15 = bf16[8,24,128]{2,1,0:T(8,128)(2,1)S(1)} async-done(((bf16[8,24,128]{2,1,0:T(8,128)(2,1)}), bf16[8,24,128]{2,1,0:T(8,128)(2,1)S(1)}, u32[]{:S(2)}, u32[]{:S(2)}) %all-to-all-start.15) | async-done | bytes 49184 | tf_op jit(solution)/shard_map/far_scatter/all_to_all | solution.py:35
  244.4 0.6 pad_maximum_fusion.3
  (49 shorter events, 0.9 us)
Async XLA Ops:
  0.0 66.8 %copy-start = (bf16[512,1024]{1,0:T(8,128)(2,1)S(1)}, bf16[512,1024]{1,0:T(8,128)(2,1)}, u32[]{:S(2)}) copy-start(bf16[512,1024]{1,0:T(8,128)(2,1)} %param.15) | copy-start | bytes 3145732
  4.7 25.5 %all-to-all-start = ((bf16[8,24,128]{2,1,0:T(8,128)(2,1)}), bf16[8,24,128]{2,1,0:T(8,128)(2,1)S(1)}, u32[]{:S(2)}, u32[]{:S(2)}) async-start(bf16[8,24,128]{2,1,0:T(8,128)(2,1)} %bitcast.103), calls=%async_computation | async-start | bytes 98304 | tf_op jit(solution)/shard_map/start_far_gather/all_to_all | solution.py:35
  18.4 2.2 copy-start.10
  18.4 2.2 copy-start.8
  30.2 13.2 %copy-start.3 = (f32[8,3,1024]{2,1,0:T(4,128)}, f32[8,3,1024]{2,1,0:T(4,128)S(1)}, u32[]{:S(2)}) copy-start(f32[8,3,1024]{2,1,0:T(4,128)S(1)} %reshape.388) | copy-start | bytes 294916
  66.9 38.7 %copy-start.4 = (f32[8,3,1024]{2,1,0:T(4,128)S(1)}, f32[8,3,1024]{2,1,0:T(4,128)}, u32[]{:S(2)}) copy-start(f32[8,3,1024]{2,1,0:T(4,128)} %copy-done.3) | copy-start | bytes 294916
  131.0 21.2 %copy-start.5 = (f32[24,1024]{1,0:T(8,128)S(1)}, f32[24,1024]{1,0:T(8,128)}, u32[]{:S(2)}) copy-start(f32[24,1024]{1,0:T(8,128)} %get-tuple-element.27) | copy-start | bytes 294916
  179.6 0.7 copy-start.1
  205.3 15.5 %copy-start.9 = (f32[3,8,128]{2,1,0:T(8,128)S(1)}, f32[3,8,128]{2,1,0:T(8,128)}, u32[]{:S(2)}) copy-start(f32[3,8,128]{2,1,0:T(8,128)} %get-tuple-element.19) | copy-start | bytes 36868
  205.3 27.2 %copy-start.2 = (bf16[8,24,1024]{2,1,0:T(8,128)(2,1)S(1)}, bf16[8,24,1024]{2,1,0:T(8,128)(2,1)}, u32[]{:S(2)}) copy-start(bf16[8,24,1024]{2,1,0:T(8,128)(2,1)} %copy-done.1) | copy-start | bytes 1179652
  216.0 28.4 %copy-start.6 = (f32[1,3,8,128]{3,2,1,0:T(8,128)S(1)}, f32[1,3,8,128]{3,2,1,0:T(8,128)}, u32[]{:S(2)}) copy-start(f32[1,3,8,128]{3,2,1,0:T(8,128)} %get-tuple-element.40) | copy-start | bytes 36868
  216.0 28.4 %copy-start.7 = (f32[1,3,8,128]{3,2,1,0:T(8,128)S(1)}, f32[1,3,8,128]{3,2,1,0:T(8,128)}, u32[]{:S(2)}) copy-start(f32[1,3,8,128]{3,2,1,0:T(8,128)} %get-tuple-element.43) | copy-start | bytes 36868
  216.0 12.3 %all-to-all-start.14 = ((bf16[8,24,1024]{2,1,0:T(8,128)(2,1)}), bf16[8,24,1024]{2,1,0:T(8,128)(2,1)S(1)}, u32[]{:S(2)}, u32[]{:S(2)}) async-start(bf16[8,24,1024]{2,1,0:T(8,128)(2,1)} %bitcast.16), calls=%async_computation.14 | async-start | bytes 786432 | tf_op jit(solution)/shard_map/near_scatter/all_to_all | solution.py:35
  229.0 15.2 %all-to-all-start.15 = ((bf16[8,24,128]{2,1,0:T(8,128)(2,1)}), bf16[8,24,128]{2,1,0:T(8,128)(2,1)S(1)}, u32[]{:S(2)}, u32[]{:S(2)}) async-start(bf16[8,24,128]{2,1,0:T(8,128)(2,1)} %reshape.380), calls=%async_computation.15 | async-start | bytes 98304 | tf_op jit(solution)/shard_map/far_scatter/all_to_all | solution.py:35

commit v5 on v4

--- a/solution.py
+++ b/solution.py
@@ -18,7 +18,7 @@
 
 
 NEAR = [
-    [owner(x, za, half(side, zh), zh) for x in range(4) for side in range(2)]
+    [owner(x, za, half(side, zh), zh) for side in range(2) for x in range(4)]
     for za in range(2)
     for zh in range(4)
 ]
@@ -40,64 +40,50 @@
 
 
 def attention_kernel(lengths_ref, x_ref, queries_ref, new_ref, cache_ref, out_ref, first_ref, spread_ref):
-    steps, _, heads, size = queries_ref.shape
+    steps, requests, heads, size = queries_ref.shape
     rows = steps * heads
     scale = size ** (-0.5)
-    wide = queries_ref[...].astype(jnp.float32).reshape(rows, size)
-    keys = cache_ref[0, 0, 0]
-    values = cache_ref[0, 0, 1]
-    scores = lax.dot_general(
-        wide.astype(jnp.bfloat16), keys, (((1,), (1,)), ((), ())), preferred_element_type=jnp.float32
-    )
-    position = lax.broadcasted_iota(jnp.int32, scores.shape, 1)
-    scores = jnp.where(position < lengths_ref[pl.program_id(0)], scores * scale, -1e30)
-    top = jnp.max(scores, axis=1, keepdims=True)
     row_step = lax.broadcasted_iota(jnp.int32, (rows, 1), 0) // heads
-    new = new_ref[...].astype(jnp.float32)
-    fresh = []
-    for step in range(steps):
-        score = jnp.sum(wide * new[step, 0, 0, 0:1], axis=1, keepdims=True) * scale
-        fresh.append(jnp.where(row_step >= step, score, -1e30))
-        top = jnp.maximum(top, fresh[-1])
-    weights = jnp.exp(scores - top)
-    total = jnp.sum(weights, axis=1, keepdims=True)
-    for step in range(steps):
-        fresh[step] = jnp.exp(fresh[step] - top)
-        total = total + fresh[step]
-    out = jnp.dot((weights / total).astype(jnp.bfloat16), values, preferred_element_type=jnp.float32)
-    for step in range(steps):
-        prob = (fresh[step] / total).astype(jnp.bfloat16).astype(jnp.float32)
-        out = out + prob * new[step, 0, 0, 1:2]
-    out_ref[...] = out.reshape(out_ref.shape)
     state = x_ref[...].astype(jnp.float32)
-    row = lax.broadcasted_iota(jnp.int32, state.shape, 0)
-    state = jnp.sum(jnp.where(row == pl.program_id(0), state, 0.0), axis=0, keepdims=True)
-    state = jnp.concatenate([state[:, k * size : (k + 1) * size] for k in range(heads)], axis=0)
-    first = state + out[:heads]
-    first_ref[0] = first
-    spread_ref[...] = jnp.broadcast_to(first.astype(jnp.bfloat16), spread_ref.shape)
+    for request in range(requests):
+        wide = queries_ref[:, request].astype(jnp.float32).reshape(rows, size)
+        keys = cache_ref[request, 0, 0]
+        values = cache_ref[request, 0, 1]
+        scores = lax.dot_general(
+            wide.astype(jnp.bfloat16), keys, (((1,), (1,)), ((), ())), preferred_element_type=jnp.float32
+        )
+        position = lax.broadcasted_iota(jnp.int32, scores.shape, 1)
+        scores = jnp.where(position < lengths_ref[request], scores * scale, -1e30)
+        top = jnp.max(scores, axis=1, keepdims=True)
+        new = new_ref[:, request, 0].astype(jnp.float32)
+        fresh = []
+        for step in range(steps):
+            score = jnp.sum(wide * new[step, 0:1], axis=1, keepdims=True) * scale
+            fresh.append(jnp.where(row_step >= step, score, -1e30))
+            top = jnp.maximum(top, fresh[-1])
+        weights = jnp.exp(scores - top)
+        total = jnp.sum(weights, axis=1, keepdims=True)
+        for step in range(steps):
+            fresh[step] = jnp.exp(fresh[step] - top)
+            total = total + fresh[step]
+        out = jnp.dot((weights / total).astype(jnp.bfloat16), values, preferred_element_type=jnp.float32)
+        for step in range(steps):
+            prob = (fresh[step] / total).astype(jnp.bfloat16).astype(jnp.float32)
+            out = out + prob * new[step, 1:2]
+        out_ref[:, request] = out.reshape(steps, heads, size)
+        row = state[request : request + 1]
+        first = jnp.concatenate([row[:, k * size : (k + 1) * size] for k in range(heads)], axis=0)
+        first = first + out[:heads]
+        first_ref[request] = first
+        spread_ref[:, request] = jnp.broadcast_to(first.astype(jnp.bfloat16), (8, heads, size))
 
 
 def attention(x_init, queries, new_kv, kv_cache, lengths):
     steps, requests, heads, size = queries.shape
-    cache_length = kv_cache.shape[3]
     out, first, spread_first = pl.pallas_call(
         attention_kernel,
-        grid_spec=pltpu.PrefetchScalarGridSpec(
-            num_scalar_prefetch=1,
-            grid=(requests,),
-            in_specs=[
-                pl.BlockSpec((requests, heads * size), lambda r, _: (0, 0)),
-                pl.BlockSpec((steps, 1, heads, size), lambda r, _: (0, r, 0, 0)),
-                pl.BlockSpec((steps, 1, 1, 2, size), lambda r, _: (0, r, 0, 0, 0)),
-                pl.BlockSpec((1, 1, 2, cache_length, size), lambda r, _: (r, 0, 0, 0, 0)),
-            ],
-            out_specs=[
-                pl.BlockSpec((steps, 1, heads, size), lambda r, _: (0, r, 0, 0)),
-                pl.BlockSpec((1, heads, size), lambda r, _: (r, 0, 0)),
-                pl.BlockSpec((8, 1, heads, size), lambda r, _: (0, r, 0, 0)),
-            ],
-        ),
+        in_specs=[pl.BlockSpec(memory_space=pltpu.SMEM)] + [pl.BlockSpec(memory_space=pltpu.VMEM)] * 4,
+        out_specs=[pl.BlockSpec(memory_space=pltpu.VMEM)] * 3,
         out_shape=[
             jax.ShapeDtypeStruct((steps, requests, heads, size), jnp.float32),
             jax.ShapeDtypeStruct((requests, heads, size), jnp.float32),

time: 246 us -> 244 us (level)
  no operation moved by 1% of the time
where the time goes in v5:
time: 244 us; the launch traced here: 243 us
  blocking collectives  177 us (73%)
  waiting for transfers between devices  24.8 us (10%)
  starting transfers between devices  21.9 us (9%)
  local copies, waits for them, and re-layouts  6.72 us (3%)
  other arithmetic  4.65 us (2%)
  matrix products  3.64 us (1%)
  Pallas kernels  3.54 us (1%)
    all_to_all x7, blocking collectives, swap(): return lax.all_to_all(array, 'r', 0, 0, axis_index_groups=group, tiled=True)  112 us
    all_to_all x6, blocking collectives, swap(): return lax.all_to_all(array, TP, 0, 0, tiled=True)  65.2 us
    all_to_all x3, waiting for transfers between devices, swap(): return lax.all_to_all(array, 'r', 0, 0, axis_index_groups=group, tiled=True)  24.8 us
    all_to_all x3, starting transfers between devices, swap(): return lax.all_to_all(array, 'r', 0, 0, axis_index_groups=group, tiled=True)  21.9 us
  transfers between devices with their start and end apart: 3, of which 3 were waited for; matrix products, arithmetic and copies ran while one was open for 2% of the time, Pallas kernels for 0%

profile of v5, /device:TPU:32, one launch (start us, length us, event | category | flops | bytes accessed | tf_op | source)
XLA Modules:
  0.0 242.6 jit_solution(6969763211275040418)
XLA Ops:
  0.0 3.5 %attention.1 = (f32[3,3,8,128]{3,2,1,0:T(8,128)}, f32[3,8,128]{2,1,0:T(8,128)}, bf16[8,3,8,128]{3,2,1,0:T(8,128)(2,1)}) custom-call(s32[3]{0:T(128)} %lengths_ref.1, bf16[3,1024]{1,0:T(4,128)(2,1)} %x_ref.1, bf16[3,3,8,128]{3,2,1,0:T(8,128)(2,1)} %queries_ref.1, bf16[3,3,1,2,128]{4,3,2,1,0:T(2,128)(2,1)} %new_ref.1, bf16[3,1,2,1024,128]{4,3,2,1,0:T(8,128)(2,1)} %cache_ref.1), custom_call_target="tpu_custom_call" | custom-call | tf_op jit(solution)/shard_map/attention/pallas_call | solution.py:83
  3.5 13.8 %all-to-all-start = ((bf16[8,24,128]{2,1,0:T(8,128)(2,1)}), bf16[8,24,128]{2,1,0:T(8,128)(2,1)S(1)}, u32[]{:S(2)}, u32[]{:S(2)}) async-start(bf16[8,24,128]{2,1,0:T(8,128)(2,1)} %bitcast.103), calls=%async_computation | async-start | bytes 98304 | tf_op jit(solution)/shard_map/start_far_gather/all_to_all | solution.py:35
  17.3 0.0 copy-start.8
  17.3 2.2 copy.36
  19.5 0.0 copy-done.10
  19.5 0.6 fusion.17
  20.1 0.1 broadcast_in_dim.101
  20.2 0.7 bitcast_select_fusion
  21.0 8.1 %all-to-all-done = bf16[8,24,128]{2,1,0:T(8,128)(2,1)S(1)} async-done(((bf16[8,24,128]{2,1,0:T(8,128)(2,1)}), bf16[8,24,128]{2,1,0:T(8,128)(2,1)S(1)}, u32[]{:S(2)}, u32[]{:S(2)}) %all-to-all-start) | async-done | bytes 49184 | tf_op jit(solution)/shard_map/start_far_gather/all_to_all | solution.py:35
  29.1 0.1 fusion.5
  29.3 12.2 %all_to_all.80 = bf16[8,24,1024]{2,1,0:T(8,128)(2,1)S(1)} all-to-all(bf16[8,24,1024]{2,1,0:T(8,128)(2,1)S(1)} %broadcast_in_dim.110), channel_id=1, replica_groups={{0,128,256,384,32,160,288,416},{8,136,264,392,40,168,296,424},{48,176,3..., dimensions={0} | all-to-all | bytes 786432 | tf_op jit(solution)/shard_map/near_gather/all_to_all | solution.py:35
  41.4 0.1 multiply_multiply_fusion.2
  41.6 0.6 convolution_convert_fusion.5
  42.3 13.8 %all_to_all.81 = bf16[8,24,1152]{2,1,0:T(8,128)(2,1)S(1)} all-to-all(bf16[8,24,1152]{2,1,0:T(8,128)(2,1)S(1)} %pad_maximum_fusion), channel_id=1, replica_groups=mesh['attn'=16,'ffn'=4,'tp'=8] {'tp'}, dimensions={0} | all-to-all | bytes 884736 | tf_op jit(solution)/shard_map/tp_scatter/all_to_all | solution.py:34
  56.0 0.1 convert_reduce_fusion.2
  56.1 0.1 slice_reduce_fusion.2
  56.2 0.1 slice_multiply_fusion.2
  56.3 9.2 %all_to_all.82 = bf16[8,24,512]{2,1,0:T(8,128)(2,1)S(1)} all-to-all(bf16[8,24,512]{2,1,0:T(8,128)(2,1)S(1)} %broadcast_in_dim.111), channel_id=1, replica_groups=mesh['attn'=16,'ffn'=4,'tp'=8] {'tp'}, dimensions={0} | all-to-all | bytes 393216 | tf_op jit(solution)/shard_map/tp_gather/all_to_all | solution.py:34
  65.6 0.4 convolution_convert_fusion.4
  66.0 11.1 %all_to_all.83 = bf16[8,24,1024]{2,1,0:T(8,128)(2,1)S(1)} all-to-all(bf16[8,24,1024]{2,1,0:T(8,128)(2,1)S(1)} %bitcast.88), channel_id=1, replica_groups={{0,128,256,384,32,160,288,416},{8,136,264,392,40,168,296,424},{48,176,3..., dimensions={0} | all-to-all | bytes 786432 | tf_op jit(solution)/shard_map/near_scatter/all_to_all | solution.py:35
  77.0 0.1 convert_reduce_fusion.6
  77.1 0.6 fusion
  77.8 27.7 %all_to_all.84 = bf16[8,24,1024]{2,1,0:T(8,128)(2,1)S(1)} all-to-all(bf16[8,24,1024]{2,1,0:T(8,128)(2,1)S(1)} %broadcast_in_dim.112), channel_id=1, replica_groups={{0,8,48,56,64,72,112,120},{32,40,16,24,96,104,80,88},{128,136,176,184,1..., dimensions={0} | all-to-all | bytes 786432 | tf_op jit(solution)/shard_map/far_exchange/all_to_all | solution.py:35
  105.5 0.1 convert_reduce_fusion.5
  105.6 0.1 multiply_convert_fusion.1
  105.7 10.9 %all_to_all.85 = bf16[8,24,1024]{2,1,0:T(8,128)(2,1)S(1)} all-to-all(bf16[8,24,1024]{2,1,0:T(8,128)(2,1)S(1)} %broadcast_in_dim.113), channel_id=1, replica_groups={{0,128,256,384,32,160,288,416},{8,136,264,392,40,168,296,424},{48,176,3..., dimensions={0} | all-to-all | bytes 786432 | tf_op jit(solution)/shard_map/near_gather/all_to_all | solution.py:35
  116.6 0.1 multiply_multiply_fusion.1
  116.7 0.6 convolution_convert_fusion.3
  117.4 11.9 %all_to_all.86 = bf16[8,24,1152]{2,1,0:T(8,128)(2,1)S(1)} all-to-all(bf16[8,24,1152]{2,1,0:T(8,128)(2,1)S(1)} %pad_maximum_fusion.1), channel_id=1, replica_groups=mesh['attn'=16,'ffn'=4,'tp'=8] {'tp'}, dimensions={0} | all-to-all | bytes 884736 | tf_op jit(solution)/shard_map/tp_scatter/all_to_all | solution.py:34
  129.3 0.1 convert_reduce_fusion.1
  129.3 0.1 slice_reduce_fusion.1
  129.4 0.1 slice_multiply_fusion.1
  129.6 9.2 %all_to_all.87 = bf16[8,24,512]{2,1,0:T(8,128)(2,1)S(1)} all-to-all(bf16[8,24,512]{2,1,0:T(8,128)(2,1)S(1)} %broadcast_in_dim.114), channel_id=1, replica_groups=mesh['attn'=16,'ffn'=4,'tp'=8] {'tp'}, dimensions={0} | all-to-all | bytes 393216 | tf_op jit(solution)/shard_map/tp_gather/all_to_all | solution.py:34
  138.8 0.4 convolution_convert_fusion.2
  139.2 11.1 %all_to_all.88 = bf16[8,24,1024]{2,1,0:T(8,128)(2,1)S(1)} all-to-all(bf16[8,24,1024]{2,1,0:T(8,128)(2,1)S(1)} %bitcast.89), channel_id=1, replica_groups={{0,128,256,384,32,160,288,416},{8,136,264,392,40,168,296,424},{48,176,3..., dimensions={0} | all-to-all | bytes 786432 | tf_op jit(solution)/shard_map/near_scatter/all_to_all | solution.py:35
  150.3 0.1 convert_reduce_fusion.4
  150.3 0.0 copy-done.5
  150.3 0.6 fusion.1
  151.0 28.0 %all_to_all.89 = bf16[8,24,1024]{2,1,0:T(8,128)(2,1)S(1)} all-to-all(bf16[8,24,1024]{2,1,0:T(8,128)(2,1)S(1)} %broadcast_in_dim.115), channel_id=1, replica_groups={{0,8,48,56,64,72,112,120},{32,40,16,24,96,104,80,88},{128,136,176,184,1..., dimensions={0} | all-to-all | bytes 786432 | tf_op jit(solution)/shard_map/far_exchange/all_to_all | solution.py:35
  179.0 0.7 copy-done.1
  179.7 0.1 convert_reduce_fusion.3
  179.8 0.1 multiply_convert_fusion
  179.9 10.6 %all_to_all.90 = bf16[8,24,1024]{2,1,0:T(8,128)(2,1)S(1)} all-to-all(bf16[8,24,1024]{2,1,0:T(8,128)(2,1)S(1)} %broadcast_in_dim.116), channel_id=1, replica_groups={{0,128,256,384,32,160,288,416},{8,136,264,392,40,168,296,424},{48,176,3..., dimensions={0} | all-to-all | bytes 786432 | tf_op jit(solution)/shard_map/near_gather/all_to_all | solution.py:35
  190.6 0.1 multiply_multiply_fusion
  190.7 0.6 convolution_convert_fusion.1
  191.3 11.9 %all_to_all.91 = bf16[8,24,1152]{2,1,0:T(8,128)(2,1)S(1)} all-to-all(bf16[8,24,1152]{2,1,0:T(8,128)(2,1)S(1)} %pad_maximum_fusion.2), channel_id=1, replica_groups=mesh['attn'=16,'ffn'=4,'tp'=8] {'tp'}, dimensions={0} | all-to-all | bytes 884736 | tf_op jit(solution)/shard_map/tp_scatter/all_to_all | solution.py:34
  203.2 0.1 convert_reduce_fusion
  203.3 0.0 copy-start.2
  203.3 0.1 slice_reduce_fusion
  203.4 0.1 slice_multiply_fusion
  203.6 9.2 %all_to_all.92 = bf16[8,24,512]{2,1,0:T(8,128)(2,1)S(1)} all-to-all(bf16[8,24,512]{2,1,0:T(8,128)(2,1)S(1)} %broadcast_in_dim.117), channel_id=1, replica_groups=mesh['attn'=16,'ffn'=4,'tp'=8] {'tp'}, dimensions={0} | all-to-all | bytes 393216 | tf_op jit(solution)/shard_map/tp_gather/all_to_all | solution.py:34
  212.8 1.1 convolution_convert_fusion
  213.9 4.9 %all-to-all-start.14 = ((bf16[8,24,1024]{2,1,0:T(8,128)(2,1)}), bf16[8,24,1024]{2,1,0:T(8,128)(2,1)S(1)}, u32[]{:S(2)}, u32[]{:S(2)}) async-start(bf16[8,24,1024]{2,1,0:T(8,128)(2,1)} %bitcast.16), calls=%async_computation.14 | async-start | bytes 786432 | tf_op jit(solution)/shard_map/near_scatter/all_to_all | solution.py:35
  218.8 0.0 copy-done.9
  218.8 7.2 %all-to-all-done.14 = bf16[8,24,1024]{2,1,0:T(8,128)(2,1)S(1)} async-done(((bf16[8,24,1024]{2,1,0:T(8,128)(2,1)}), bf16[8,24,1024]{2,1,0:T(8,128)(2,1)S(1)}, u32[]{:S(2)}, u32[]{:S(2)}) %all-to-all-start.14) | async-done | bytes 393248 | tf_op jit(solution)/shard_map/near_scatter/all_to_all | solution.py:35
  226.0 0.1 reduce_sum.147
  226.1 0.7 reshape.380
  226.8 3.3 %all-to-all-start.15 = ((bf16[8,24,128]{2,1,0:T(8,128)(2,1)}), bf16[8,24,128]{2,1,0:T(8,128)(2,1)S(1)}, u32[]{:S(2)}, u32[]{:S(2)}) async-start(bf16[8,24,128]{2,1,0:T(8,128)(2,1)} %reshape.380), calls=%async_computation.15 | async-start | bytes 98304 | tf_op jit(solution)/shard_map/far_scatter/all_to_all | solution.py:35
  230.2 0.2 copy.29
  230.4 0.2 copy.25
  230.7 0.8 constant_dynamic-slice_fusion
  231.5 0.8 constant_dynamic-slice_fusion.1
  232.4 9.5 %all-to-all-done.15 = bf16[8,24,128]{2,1,0:T(8,128)(2,1)S(1)} async-done(((bf16[8,24,128]{2,1,0:T(8,128)(2,1)}), bf16[8,24,128]{2,1,0:T(8,128)(2,1)S(1)}, u32[]{:S(2)}, u32[]{:S(2)}) %all-to-all-start.15) | async-done | bytes 49184 | tf_op jit(solution)/shard_map/far_scatter/all_to_all | solution.py:35
  241.9 0.6 pad_maximum_fusion.3
  (49 shorter events, 0.9 us)
Async XLA Ops:
  0.0 65.6 %copy-start = (bf16[512,1024]{1,0:T(8,128)(2,1)S(1)}, bf16[512,1024]{1,0:T(8,128)(2,1)}, u32[]{:S(2)}) copy-start(bf16[512,1024]{1,0:T(8,128)(2,1)} %param.15) | copy-start | bytes 3145732
  3.5 25.5 %all-to-all-start = ((bf16[8,24,128]{2,1,0:T(8,128)(2,1)}), bf16[8,24,128]{2,1,0:T(8,128)(2,1)S(1)}, u32[]{:S(2)}, u32[]{:S(2)}) async-start(bf16[8,24,128]{2,1,0:T(8,128)(2,1)} %bitcast.103), calls=%async_computation | async-start | bytes 98304 | tf_op jit(solution)/shard_map/start_far_gather/all_to_all | solution.py:35
  17.3 2.2 copy-start.10
  17.3 2.2 copy-start.8
  29.1 13.1 %copy-start.3 = (f32[8,3,1024]{2,1,0:T(4,128)}, f32[8,3,1024]{2,1,0:T(4,128)S(1)}, u32[]{:S(2)}) copy-start(f32[8,3,1024]{2,1,0:T(4,128)S(1)} %reshape.388) | copy-start | bytes 294916
  65.6 40.0 %copy-start.4 = (f32[8,3,1024]{2,1,0:T(4,128)S(1)}, f32[8,3,1024]{2,1,0:T(4,128)}, u32[]{:S(2)}) copy-start(f32[8,3,1024]{2,1,0:T(4,128)} %copy-done.3) | copy-start | bytes 294916
  129.2 21.1 %copy-start.5 = (f32[24,1024]{1,0:T(8,128)S(1)}, f32[24,1024]{1,0:T(8,128)}, u32[]{:S(2)}) copy-start(f32[24,1024]{1,0:T(8,128)} %get-tuple-element.27) | copy-start | bytes 294916
  179.0 0.7 copy-start.1
  203.2 15.6 %copy-start.9 = (f32[3,8,128]{2,1,0:T(8,128)S(1)}, f32[3,8,128]{2,1,0:T(8,128)}, u32[]{:S(2)}) copy-start(f32[3,8,128]{2,1,0:T(8,128)} %get-tuple-element.19) | copy-start | bytes 36868
  203.3 26.9 %copy-start.2 = (bf16[8,24,1024]{2,1,0:T(8,128)(2,1)S(1)}, bf16[8,24,1024]{2,1,0:T(8,128)(2,1)}, u32[]{:S(2)}) copy-start(bf16[8,24,1024]{2,1,0:T(8,128)(2,1)} %copy-done.1) | copy-start | bytes 1179652
  213.9 27.9 %copy-start.6 = (f32[1,3,8,128]{3,2,1,0:T(8,128)S(1)}, f32[1,3,8,128]{3,2,1,0:T(8,128)}, u32[]{:S(2)}) copy-start(f32[1,3,8,128]{3,2,1,0:T(8,128)} %get-tuple-element.40) | copy-start | bytes 36868
  213.9 28.0 %copy-start.7 = (f32[1,3,8,128]{3,2,1,0:T(8,128)S(1)}, f32[1,3,8,128]{3,2,1,0:T(8,128)}, u32[]{:S(2)}) copy-start(f32[1,3,8,128]{3,2,1,0:T(8,128)} %get-tuple-element.43) | copy-start | bytes 36868
  213.9 12.1 %all-to-all-start.14 = ((bf16[8,24,1024]{2,1,0:T(8,128)(2,1)}), bf16[8,24,1024]{2,1,0:T(8,128)(2,1)S(1)}, u32[]{:S(2)}, u32[]{:S(2)}) async-start(bf16[8,24,1024]{2,1,0:T(8,128)(2,1)} %bitcast.16), calls=%async_computation.14 | async-start | bytes 786432 | tf_op jit(solution)/shard_map/near_scatter/all_to_all | solution.py:35
  226.8 15.0 %all-to-all-start.15 = ((bf16[8,24,128]{2,1,0:T(8,128)(2,1)}), bf16[8,24,128]{2,1,0:T(8,128)(2,1)S(1)}, u32[]{:S(2)}, u32[]{:S(2)}) async-start(bf16[8,24,128]{2,1,0:T(8,128)(2,1)} %reshape.380), calls=%async_computation.15 | async-start | bytes 98304 | tf_op jit(solution)/shard_map/far_scatter/all_to_all | solution.py:35

commit v6 on v5

--- a/solution.py
+++ b/solution.py
@@ -18,7 +18,7 @@
 
 
 NEAR = [
-    [owner(x, za, half(side, zh), zh) for side in range(2) for x in range(4)]
+    [owner(x, za, half(side, zh), zh) for side in range(2) for x in (0, 2, 1, 3)]
     for za in range(2)
     for zh in range(4)
 ]

time: 244 us -> 244 us (level)
  no operation moved by 1% of the time
where the time goes in v6:
time: 244 us; the launch traced here: 243 us
  blocking collectives  177 us (73%)
  waiting for transfers between devices  24.9 us (10%)
  starting transfers between devices  21.9 us (9%)
  local copies, waits for them, and re-layouts  6.72 us (3%)
  other arithmetic  4.65 us (2%)
  matrix products  3.65 us (1%)
  Pallas kernels  3.54 us (1%)
    all_to_all x7, blocking collectives, swap(): return lax.all_to_all(array, 'r', 0, 0, axis_index_groups=group, tiled=True)  112 us
    all_to_all x6, blocking collectives, swap(): return lax.all_to_all(array, TP, 0, 0, tiled=True)  65.2 us
    all_to_all x3, waiting for transfers between devices, swap(): return lax.all_to_all(array, 'r', 0, 0, axis_index_groups=group, tiled=True)  24.9 us
    all_to_all x3, starting transfers between devices, swap(): return lax.all_to_all(array, 'r', 0, 0, axis_index_groups=group, tiled=True)  21.9 us
  transfers between devices with their start and end apart: 3, of which 3 were waited for; matrix products, arithmetic and copies ran while one was open for 2% of the time, Pallas kernels for 0%

profile of v6, /device:TPU:32, one launch (start us, length us, event | category | flops | bytes accessed | tf_op | source)
XLA Modules:
  0.0 242.7 jit_solution(2794614725959224505)
XLA Ops:
  0.0 0.0 copy-start
  0.0 3.5 %attention.1 = (f32[3,3,8,128]{3,2,1,0:T(8,128)}, f32[3,8,128]{2,1,0:T(8,128)}, bf16[8,3,8,128]{3,2,1,0:T(8,128)(2,1)}) custom-call(s32[3]{0:T(128)} %lengths_ref.1, bf16[3,1024]{1,0:T(4,128)(2,1)} %x_ref.1, bf16[3,3,8,128]{3,2,1,0:T(8,128)(2,1)} %queries_ref.1, bf16[3,3,1,2,128]{4,3,2,1,0:T(2,128)(2,1)} %new_ref.1, bf16[3,1,2,1024,128]{4,3,2,1,0:T(8,128)(2,1)} %cache_ref.1), custom_call_target="tpu_custom_call" | custom-call | tf_op jit(solution)/shard_map/attention/pallas_call | solution.py:83
  3.5 13.8 %all-to-all-start = ((bf16[8,24,128]{2,1,0:T(8,128)(2,1)}), bf16[8,24,128]{2,1,0:T(8,128)(2,1)S(1)}, u32[]{:S(2)}, u32[]{:S(2)}) async-start(bf16[8,24,128]{2,1,0:T(8,128)(2,1)} %bitcast.103), calls=%async_computation | async-start | bytes 98304 | tf_op jit(solution)/shard_map/start_far_gather/all_to_all | solution.py:35
  17.3 0.0 copy-start.8
  17.3 2.2 copy.36
  19.5 0.0 copy-done.10
  19.5 0.0 copy-done.8
  19.5 0.6 fusion.17
  20.1 0.1 broadcast_in_dim.101
  20.2 0.7 bitcast_select_fusion
  21.0 8.1 %all-to-all-done = bf16[8,24,128]{2,1,0:T(8,128)(2,1)S(1)} async-done(((bf16[8,24,128]{2,1,0:T(8,128)(2,1)}), bf16[8,24,128]{2,1,0:T(8,128)(2,1)S(1)}, u32[]{:S(2)}, u32[]{:S(2)}) %all-to-all-start) | async-done | bytes 49184 | tf_op jit(solution)/shard_map/start_far_gather/all_to_all | solution.py:35
  29.1 0.1 fusion.5
  29.3 12.2 %all_to_all.80 = bf16[8,24,1024]{2,1,0:T(8,128)(2,1)S(1)} all-to-all(bf16[8,24,1024]{2,1,0:T(8,128)(2,1)S(1)} %broadcast_in_dim.110), channel_id=1, replica_groups={{0,256,128,384,32,288,160,416},{8,264,136,392,40,296,168,424},{48,304,1..., dimensions={0} | all-to-all | bytes 786432 | tf_op jit(solution)/shard_map/near_gather/all_to_all | solution.py:35
  41.4 0.1 multiply_multiply_fusion.2
  41.6 0.6 convolution_convert_fusion.5
  42.2 13.8 %all_to_all.81 = bf16[8,24,1152]{2,1,0:T(8,128)(2,1)S(1)} all-to-all(bf16[8,24,1152]{2,1,0:T(8,128)(2,1)S(1)} %pad_maximum_fusion), channel_id=1, replica_groups=mesh['attn'=16,'ffn'=4,'tp'=8] {'tp'}, dimensions={0} | all-to-all | bytes 884736 | tf_op jit(solution)/shard_map/tp_scatter/all_to_all | solution.py:34
  56.0 0.1 convert_reduce_fusion.2
  56.1 0.1 slice_reduce_fusion.2
  56.2 0.1 slice_multiply_fusion.2
  56.3 9.2 %all_to_all.82 = bf16[8,24,512]{2,1,0:T(8,128)(2,1)S(1)} all-to-all(bf16[8,24,512]{2,1,0:T(8,128)(2,1)S(1)} %broadcast_in_dim.111), channel_id=1, replica_groups=mesh['attn'=16,'ffn'=4,'tp'=8] {'tp'}, dimensions={0} | all-to-all | bytes 393216 | tf_op jit(solution)/shard_map/tp_gather/all_to_all | solution.py:34
  65.6 0.4 convolution_convert_fusion.4
  66.0 11.0 %all_to_all.83 = bf16[8,24,1024]{2,1,0:T(8,128)(2,1)S(1)} all-to-all(bf16[8,24,1024]{2,1,0:T(8,128)(2,1)S(1)} %bitcast.88), channel_id=1, replica_groups={{0,256,128,384,32,288,160,416},{8,264,136,392,40,296,168,424},{48,304,1..., dimensions={0} | all-to-all | bytes 786432 | tf_op jit(solution)/shard_map/near_scatter/all_to_all | solution.py:35
  77.0 0.1 convert_reduce_fusion.6
  77.0 0.6 fusion
  77.7 28.0 %all_to_all.84 = bf16[8,24,1024]{2,1,0:T(8,128)(2,1)S(1)} all-to-all(bf16[8,24,1024]{2,1,0:T(8,128)(2,1)S(1)} %broadcast_in_dim.112), channel_id=1, replica_groups={{0,8,48,56,64,72,112,120},{32,40,16,24,96,104,80,88},{128,136,176,184,1..., dimensions={0} | all-to-all | bytes 786432 | tf_op jit(solution)/shard_map/far_exchange/all_to_all | solution.py:35
  105.7 0.1 convert_reduce_fusion.5
  105.7 0.1 multiply_convert_fusion.1
  105.8 10.8 %all_to_all.85 = bf16[8,24,1024]{2,1,0:T(8,128)(2,1)S(1)} all-to-all(bf16[8,24,1024]{2,1,0:T(8,128)(2,1)S(1)} %broadcast_in_dim.113), channel_id=1, replica_groups={{0,256,128,384,32,288,160,416},{8,264,136,392,40,296,168,424},{48,304,1..., dimensions={0} | all-to-all | bytes 786432 | tf_op jit(solution)/shard_map/near_gather/all_to_all | solution.py:35
  116.7 0.1 multiply_multiply_fusion.1
  116.8 0.6 convolution_convert_fusion.3
  117.5 11.9 %all_to_all.86 = bf16[8,24,1152]{2,1,0:T(8,128)(2,1)S(1)} all-to-all(bf16[8,24,1152]{2,1,0:T(8,128)(2,1)S(1)} %pad_maximum_fusion.1), channel_id=1, replica_groups=mesh['attn'=16,'ffn'=4,'tp'=8] {'tp'}, dimensions={0} | all-to-all | bytes 884736 | tf_op jit(solution)/shard_map/tp_scatter/all_to_all | solution.py:34
  129.3 0.1 convert_reduce_fusion.1
  129.4 0.1 slice_reduce_fusion.1
  129.5 0.1 slice_multiply_fusion.1
  129.7 9.2 %all_to_all.87 = bf16[8,24,512]{2,1,0:T(8,128)(2,1)S(1)} all-to-all(bf16[8,24,512]{2,1,0:T(8,128)(2,1)S(1)} %broadcast_in_dim.114), channel_id=1, replica_groups=mesh['attn'=16,'ffn'=4,'tp'=8] {'tp'}, dimensions={0} | all-to-all | bytes 393216 | tf_op jit(solution)/shard_map/tp_gather/all_to_all | solution.py:34
  138.9 0.4 convolution_convert_fusion.2
  139.3 11.0 %all_to_all.88 = bf16[8,24,1024]{2,1,0:T(8,128)(2,1)S(1)} all-to-all(bf16[8,24,1024]{2,1,0:T(8,128)(2,1)S(1)} %bitcast.89), channel_id=1, replica_groups={{0,256,128,384,32,288,160,416},{8,264,136,392,40,296,168,424},{48,304,1..., dimensions={0} | all-to-all | bytes 786432 | tf_op jit(solution)/shard_map/near_scatter/all_to_all | solution.py:35
  150.3 0.1 convert_reduce_fusion.4
  150.4 0.6 fusion.1
  151.0 28.2 %all_to_all.89 = bf16[8,24,1024]{2,1,0:T(8,128)(2,1)S(1)} all-to-all(bf16[8,24,1024]{2,1,0:T(8,128)(2,1)S(1)} %broadcast_in_dim.115), channel_id=1, replica_groups={{0,8,48,56,64,72,112,120},{32,40,16,24,96,104,80,88},{128,136,176,184,1..., dimensions={0} | all-to-all | bytes 786432 | tf_op jit(solution)/shard_map/far_exchange/all_to_all | solution.py:35
  179.2 0.7 copy-done.1
  180.0 0.1 convert_reduce_fusion.3
  180.0 0.1 multiply_convert_fusion
  180.1 10.6 %all_to_all.90 = bf16[8,24,1024]{2,1,0:T(8,128)(2,1)S(1)} all-to-all(bf16[8,24,1024]{2,1,0:T(8,128)(2,1)S(1)} %broadcast_in_dim.116), channel_id=1, replica_groups={{0,256,128,384,32,288,160,416},{8,264,136,392,40,296,168,424},{48,304,1..., dimensions={0} | all-to-all | bytes 786432 | tf_op jit(solution)/shard_map/near_gather/all_to_all | solution.py:35
  190.8 0.1 multiply_multiply_fusion
  190.9 0.6 convolution_convert_fusion.1
  191.6 11.9 %all_to_all.91 = bf16[8,24,1152]{2,1,0:T(8,128)(2,1)S(1)} all-to-all(bf16[8,24,1152]{2,1,0:T(8,128)(2,1)S(1)} %pad_maximum_fusion.2), channel_id=1, replica_groups=mesh['attn'=16,'ffn'=4,'tp'=8] {'tp'}, dimensions={0} | all-to-all | bytes 884736 | tf_op jit(solution)/shard_map/tp_scatter/all_to_all | solution.py:34
  203.4 0.1 convert_reduce_fusion
  203.5 0.1 slice_reduce_fusion
  203.6 0.1 slice_multiply_fusion
  203.8 9.2 %all_to_all.92 = bf16[8,24,512]{2,1,0:T(8,128)(2,1)S(1)} all-to-all(bf16[8,24,512]{2,1,0:T(8,128)(2,1)S(1)} %broadcast_in_dim.117), channel_id=1, replica_groups=mesh['attn'=16,'ffn'=4,'tp'=8] {'tp'}, dimensions={0} | all-to-all | bytes 393216 | tf_op jit(solution)/shard_map/tp_gather/all_to_all | solution.py:34
  213.0 1.1 convolution_convert_fusion
  214.1 4.8 %all-to-all-start.14 = ((bf16[8,24,1024]{2,1,0:T(8,128)(2,1)}), bf16[8,24,1024]{2,1,0:T(8,128)(2,1)S(1)}, u32[]{:S(2)}, u32[]{:S(2)}) async-start(bf16[8,24,1024]{2,1,0:T(8,128)(2,1)} %bitcast.16), calls=%async_computation.14 | async-start | bytes 786432 | tf_op jit(solution)/shard_map/near_scatter/all_to_all | solution.py:35
  218.9 0.0 copy-done.9
  219.0 7.2 %all-to-all-done.14 = bf16[8,24,1024]{2,1,0:T(8,128)(2,1)S(1)} async-done(((bf16[8,24,1024]{2,1,0:T(8,128)(2,1)}), bf16[8,24,1024]{2,1,0:T(8,128)(2,1)S(1)}, u32[]{:S(2)}, u32[]{:S(2)}) %all-to-all-start.14) | async-done | bytes 393248 | tf_op jit(solution)/shard_map/near_scatter/all_to_all | solution.py:35
  226.2 0.1 reduce_sum.147
  226.3 0.7 reshape.380
  227.0 3.3 %all-to-all-start.15 = ((bf16[8,24,128]{2,1,0:T(8,128)(2,1)}), bf16[8,24,128]{2,1,0:T(8,128)(2,1)S(1)}, u32[]{:S(2)}, u32[]{:S(2)}) async-start(bf16[8,24,128]{2,1,0:T(8,128)(2,1)} %reshape.380), calls=%async_computation.15 | async-start | bytes 98304 | tf_op jit(solution)/shard_map/far_scatter/all_to_all | solution.py:35
  230.3 0.2 copy.29
  230.5 0.2 copy.25
  230.9 0.8 constant_dynamic-slice_fusion
  231.7 0.8 constant_dynamic-slice_fusion.1
  232.5 9.5 %all-to-all-done.15 = bf16[8,24,128]{2,1,0:T(8,128)(2,1)S(1)} async-done(((bf16[8,24,128]{2,1,0:T(8,128)(2,1)}), bf16[8,24,128]{2,1,0:T(8,128)(2,1)S(1)}, u32[]{:S(2)}, u32[]{:S(2)}) %all-to-all-start.15) | async-done | bytes 49184 | tf_op jit(solution)/shard_map/far_scatter/all_to_all | solution.py:35
  242.1 0.6 pad_maximum_fusion.3
  (49 shorter events, 0.9 us)
Async XLA Ops:
  0.0 65.6 %copy-start = (bf16[512,1024]{1,0:T(8,128)(2,1)S(1)}, bf16[512,1024]{1,0:T(8,128)(2,1)}, u32[]{:S(2)}) copy-start(bf16[512,1024]{1,0:T(8,128)(2,1)} %param.15) | copy-start | bytes 3145732
  3.5 25.5 %all-to-all-start = ((bf16[8,24,128]{2,1,0:T(8,128)(2,1)}), bf16[8,24,128]{2,1,0:T(8,128)(2,1)S(1)}, u32[]{:S(2)}, u32[]{:S(2)}) async-start(bf16[8,24,128]{2,1,0:T(8,128)(2,1)} %bitcast.103), calls=%async_computation | async-start | bytes 98304 | tf_op jit(solution)/shard_map/start_far_gather/all_to_all | solution.py:35
  17.3 2.2 copy-start.10
  17.3 2.2 copy-start.8
  29.1 13.1 %copy-start.3 = (f32[8,3,1024]{2,1,0:T(4,128)}, f32[8,3,1024]{2,1,0:T(4,128)S(1)}, u32[]{:S(2)}) copy-start(f32[8,3,1024]{2,1,0:T(4,128)S(1)} %reshape.388) | copy-start | bytes 294916
  65.6 40.2 %copy-start.4 = (f32[8,3,1024]{2,1,0:T(4,128)S(1)}, f32[8,3,1024]{2,1,0:T(4,128)}, u32[]{:S(2)}) copy-start(f32[8,3,1024]{2,1,0:T(4,128)} %copy-done.3) | copy-start | bytes 294916
  129.3 21.0 %copy-start.5 = (f32[24,1024]{1,0:T(8,128)S(1)}, f32[24,1024]{1,0:T(8,128)}, u32[]{:S(2)}) copy-start(f32[24,1024]{1,0:T(8,128)} %get-tuple-element.27) | copy-start | bytes 294916
  179.2 0.7 copy-start.1
  203.4 15.5 %copy-start.9 = (f32[3,8,128]{2,1,0:T(8,128)S(1)}, f32[3,8,128]{2,1,0:T(8,128)}, u32[]{:S(2)}) copy-start(f32[3,8,128]{2,1,0:T(8,128)} %get-tuple-element.19) | copy-start | bytes 36868
  203.5 26.8 %copy-start.2 = (bf16[8,24,1024]{2,1,0:T(8,128)(2,1)S(1)}, bf16[8,24,1024]{2,1,0:T(8,128)(2,1)}, u32[]{:S(2)}) copy-start(bf16[8,24,1024]{2,1,0:T(8,128)(2,1)} %copy-done.1) | copy-start | bytes 1179652
  214.1 27.9 %copy-start.6 = (f32[1,3,8,128]{3,2,1,0:T(8,128)S(1)}, f32[1,3,8,128]{3,2,1,0:T(8,128)}, u32[]{:S(2)}) copy-start(f32[1,3,8,128]{3,2,1,0:T(8,128)} %get-tuple-element.40) | copy-start | bytes 36868
  214.1 27.9 %copy-start.7 = (f32[1,3,8,128]{3,2,1,0:T(8,128)S(1)}, f32[1,3,8,128]{3,2,1,0:T(8,128)}, u32[]{:S(2)}) copy-start(f32[1,3,8,128]{3,2,1,0:T(8,128)} %get-tuple-element.43) | copy-start | bytes 36868
  214.1 12.0 %all-to-all-start.14 = ((bf16[8,24,1024]{2,1,0:T(8,128)(2,1)}), bf16[8,24,1024]{2,1,0:T(8,128)(2,1)S(1)}, u32[]{:S(2)}, u32[]{:S(2)}) async-start(bf16[8,24,1024]{2,1,0:T(8,128)(2,1)} %bitcast.16), calls=%async_computation.14 | async-start | bytes 786432 | tf_op jit(solution)/shard_map/near_scatter/all_to_all | solution.py:35
  227.0 15.1 %all-to-all-start.15 = ((bf16[8,24,128]{2,1,0:T(8,128)(2,1)}), bf16[8,24,128]{2,1,0:T(8,128)(2,1)S(1)}, u32[]{:S(2)}, u32[]{:S(2)}) async-start(bf16[8,24,128]{2,1,0:T(8,128)(2,1)} %reshape.380), calls=%async_computation.15 | async-start | bytes 98304 | tf_op jit(solution)/shard_map/far_scatter/all_to_all | solution.py:35
